TPU v7x, 256 devices: a whole 4x4x8 slice. The times are simulated.
256 devices in a mesh: seq: 64 (over y, z, x_lo), chan: 4 (over x_hi, core).
Axes of the slice: x: 4 (x_hi: 2, x_lo: 2; x = x_hi * 2 + x_lo), y: 4, z: 8, core: 2. Of those that a mesh axis runs over, the one named last changes fastest.
Arguments:
- inputs: bfloat16 [2, 65536, 2048], P(None, 'seq', 'chan'), may hold values from -6 to 6
- mix_first: bfloat16 [256, 256, 256], P('seq'), may hold values from -0.375 to 0.375
- mix_second: bfloat16 [256, 256, 256], P('seq'), may hold values from -0.375 to 0.375
- gate_scale: float32 [2048], P('chan'), may hold values from 0.5 to 2
- gate_bias: float32 [2048], P('chan'), may hold values from -3 to 3
- up_first: bfloat16 [4, 512, 512], P('chan'), may hold values from -0.25 to 0.25
- up_second: bfloat16 [4, 2048, 512], P('chan'), may hold values from -0.25 to 0.25
- down_first: bfloat16 [4, 512, 2048], P('chan'), may hold values from -0.125 to 0.125
- down_second: bfloat16 [4, 512, 512], P('chan'), may hold values from -0.25 to 0.25
Outputs:
- layer_out: bfloat16 [2, 65536, 2048], P(None, ('seq', 'chan'))
All inputs are finite; a program needn't handle non-finite values.
Results may differ from a plain program's by a relative error of at most 0.008.
Values may be sent and summed in bfloat16 or wider, within the bound.
No kernel may reach another device: no remote copies, remote signals or barrier semaphores. Data moves between devices by JAX's collectives and lax.ppermute only.
A program may use at most 128 MiB of HBM per device.

v0:
```python
import jax
import jax.numpy as jnp
from jax import lax
from jax.sharding import PartitionSpec as P


def shard_monarch(values, inner_weight, outer_weight):
    chan_count = lax.axis_size("chan")
    inner_width = inner_weight.shape[1]
    out_width = outer_weight.shape[1]
    sub_width = inner_width // chan_count
    seq_count, row_count = (values.shape[0], values.shape[1])
    inner_rows = jnp.einsum(
        "qp,stp->stq", inner_weight[0], values, preferred_element_type=jnp.float32
    )
    inner_rows = inner_rows.astype(jnp.bfloat16).reshape(
        seq_count, row_count, chan_count, sub_width
    )
    permuted = lax.all_to_all(inner_rows, "chan", split_axis=2, concat_axis=2, tiled=True)
    outer_blocks = outer_weight[0].reshape(out_width, sub_width, chan_count)
    return jnp.einsum("oqc,stcq->sto", outer_blocks, permuted, preferred_element_type=jnp.float32)


def on_device(
    inputs,
    mix_first,
    mix_second,
    gate_scale,
    gate_bias,
    up_first,
    up_second,
    down_first,
    down_second,
):
    seq_count, row_count, chan_width = inputs.shape
    blocks_here = mix_first.shape[0]
    group_width = mix_first.shape[1]
    grouped = inputs.reshape(seq_count, blocks_here, group_width, chan_width)
    first_pass = jnp.einsum(
        "abq,saqc->sabc", mix_first, grouped, preferred_element_type=jnp.float32
    ).astype(jnp.bfloat16)
    mixed_rows = jnp.einsum(
        "bxy,sybc->sxbc",
        mix_second,
        lax.all_to_all(first_pass, "seq", split_axis=2, concat_axis=1, tiled=True),
        preferred_element_type=jnp.float32,
    ).astype(jnp.bfloat16)
    restored = lax.all_to_all(mixed_rows, "seq", split_axis=1, concat_axis=2, tiled=True).reshape(
        seq_count, row_count, chan_width
    )
    residual_in = inputs.astype(jnp.float32)
    hidden = (
        residual_in
        + restored.astype(jnp.float32) * jax.nn.sigmoid(gate_scale * residual_in + gate_bias)
    ).astype(jnp.bfloat16)
    expanded = shard_monarch(hidden, up_first, up_second)
    activated = jax.nn.gelu(expanded, approximate=True).astype(jnp.bfloat16)
    contracted = shard_monarch(activated, down_first, down_second)
    result = (hidden.astype(jnp.float32) + contracted).astype(jnp.bfloat16)
    return lax.all_to_all(result, "chan", split_axis=1, concat_axis=2, tiled=True)


def solution(mesh):
    return jax.shard_map(
        on_device,
        mesh=mesh,
        in_specs=(
            P(None, "seq", "chan"),
            P("seq", None, None),
            P("seq", None, None),
            P("chan"),
            P("chan"),
            P("chan", None, None),
            P("chan", None, None),
            P("chan", None, None),
            P("chan", None, None),
        ),
        out_specs=P(None, ("seq", "chan"), None),
        check_vma=False,
    )
```

profile of v0, /device:TPU:1, one launch (start us, length us, event | category | flops | bytes accessed | tf_op | source)
XLA Modules:
  0.0 288.9 jit_solution(14735267536404560936)
XLA Ops:
  0.0 4.1 %convert_bitcast_fusion.1 = bf16[2,4,256,512]{2,3,0,1:T(8,128)(2,1)} fusion(bf16[2,4,256,512]{3,2,1,0:T(8,128)(2,1)} %bitcast.59, bf16[4,256,256]{2,1,0:T(8,128)(2,1)} %param.10), kind=kOutput, calls=%fused_computation.30 | convolution fusion | flops 537919488 | bytes 4718592 | tf_op jit(solution)/shard_map/abq,saqc->sabc/dot_general | solution.py:39
  4.1 6.2 %copy.50 = bf16[2,4,256,512]{3,0,1,2:T(2,128)(2,1)} copy(bf16[2,4,256,512]{2,3,0,1:T(8,128)(2,1)} %convert_bitcast_fusion.1) | data formatting | bytes 4194304 | tf_op jit(solution)/shard_map/convert_element_type | solution.py:41
  10.3 63.2 %all_to_all.55 = bf16[2,4,256,512]{3,0,1,2:T(2,128)(2,1)S(1)} all-to-all(bf16[2,4,256,512]{3,0,1,2:T(2,128)(2,1)} %copy.50), channel_id=1, replica_groups=mesh['seq'=64,'chan'=4] {'seq'}, dimensions={2} | all-to-all | bytes 4194304 | tf_op jit(solution)/shard_map/all_to_all | solution.py:45
  73.5 0.8 copy.51
  74.3 0.0 copy-start.3
  74.3 1.3 copy.52
  75.6 2.4 convert_bitcast_fusion
  78.0 6.2 %copy.54 = bf16[2,256,4,512]{3,0,2,1:T(2,128)(2,1)} copy(bf16[2,256,4,512]{1,3,0,2:T(8,128)(2,1)} %convert_bitcast_fusion) | data formatting | bytes 4194304 | tf_op jit(solution)/shard_map/convert_element_type | solution.py:47
  84.2 56.1 %all_to_all.56 = bf16[2,256,4,512]{3,0,2,1:T(2,128)(2,1)S(1)} all-to-all(bf16[2,256,4,512]{3,0,2,1:T(2,128)(2,1)} %copy.54), channel_id=1, replica_groups=mesh['seq'=64,'chan'=4] {'seq'}, dimensions={1} | all-to-all | bytes 4194304 | tf_op jit(solution)/shard_map/all_to_all | solution.py:48
  140.3 0.7 copy_convert_fusion
  141.0 2.7 copy.56
  143.7 2.8 copy.57
  146.5 5.3 %reshape.20 = f32[2,1024,512]{2,1,0:T(8,128)} reshape(f32[2,4,64,4,512]{4,3,2,1,0:T(4,128)} %copy.57) | data formatting | bytes 8388608 | tf_op jit(solution)/shard_map/convert_element_type | solution.py:54
  151.9 4.3 %fusion.17 = bf16[2,1024,512]{2,1,0:T(8,128)(2,1)S(1)} fusion(f32[2,1024,512]{2,1,0:T(8,128)} %reshape.20, bf16[2,1024,512]{2,1,0:T(8,128)(2,1)} %param.9, f32[512]{0:T(512)S(1)} %copy-done.5, f32[512]{0:T(512)S(1)} %copy-done.6), kind=kLoop, calls=%fused_computation.20 | loop fusion | flops 9437184 | bytes 8392704 | tf_op jit(solution)/shard_map/convert_element_type | solution.py:55
  156.2 0.0 copy-start.2
  156.2 2.6 convolution_convert_fusion
  158.8 3.9 %copy.58 = bf16[2,1024,4,128]{3,1,0,2:T(8,128)(2,1)} copy(bf16[2,1024,4,128]{1,3,2,0:T(8,128)(2,1)} %bitcast.62) | data formatting | bytes 4194304 | tf_op jit(solution)/shard_map/reshape | solution.py:16
  162.8 7.7 %all-to-all-start.2 = ((bf16[2,1024,4,128]{3,1,0,2:T(8,128)(2,1)}), bf16[2,1024,4,128]{3,1,0,2:T(8,128)(2,1)}, u32[]{:S(2)}, u32[]{:S(2)}) async-start(bf16[2,1024,4,128]{3,1,0,2:T(8,128)(2,1)} %copy.58), calls=%async_computation.2 | async-start | bytes 4194304 | tf_op jit(solution)/shard_map/all_to_all | solution.py:19
  170.4 4.0 %copy.59 = bf16[1,2048,512]{1,2,0:T(8,128)(2,1)} copy(bf16[1,2048,512]{2,1,0:T(8,128)(2,1)} %param.15) | data formatting | bytes 4194304 | tf_op args[6]
  174.4 4.1 %reshape_squeeze.6 = bf16[2048,128,4]{0,2,1:T(4,128)(2,1)} reshape(bf16[1,2048,512]{1,2,0:T(8,128)(2,1)} %copy.59) | data formatting | bytes 4194304 | tf_op jit(solution)/shard_map/reshape;squeeze | solution.py:20
  178.5 18.4 %all-to-all-done.2 = bf16[2,1024,4,128]{3,1,0,2:T(8,128)(2,1)} async-done(((bf16[2,1024,4,128]{3,1,0,2:T(8,128)(2,1)}), bf16[2,1024,4,128]{3,1,0,2:T(8,128)(2,1)}, u32[]{:S(2)}, u32[]{:S(2)}) %all-to-all-start.2) | async-done | bytes 2097184 | tf_op jit(solution)/shard_map/all_to_all | solution.py:19
  196.9 15.2 %fusion.27 = bf16[2,1024,512]{1,2,0:T(8,128)(2,1)} fusion(bf16[1,512,2048]{2,1,0:T(8,128)(2,1)S(1)} %copy-done, bf16[2,1024,4,128]{3,1,0,2:T(8,128)(2,1)} %all-to-all-done.2, bf16[2048,128,4,1]{0,2,1,3:T(4,128)(2,1)} %bitcast.60), kind=kOutput, calls=%fused_computation.31 | convolution fusion | flops 8628731904 | bytes 8388608 | tf_op jit(solution)/shard_map/qp,stp->stq/dot_general | solution.py:13
  212.1 4.0 %copy.61 = bf16[2,1024,4,128]{3,1,0,2:T(8,128)(2,1)} copy(bf16[2,1024,4,128]{1,3,2,0:T(8,128)(2,1)} %bitcast.61) | data formatting | bytes 4194304 | tf_op jit(solution)/shard_map/reshape | solution.py:16
  216.1 4.6 %all-to-all-start.3 = ((bf16[2,1024,4,128]{3,1,0,2:T(8,128)(2,1)}), bf16[2,1024,4,128]{3,1,0,2:T(8,128)(2,1)S(1)}, u32[]{:S(2)}, u32[]{:S(2)}) async-start(bf16[2,1024,4,128]{3,1,0,2:T(8,128)(2,1)} %copy.61), calls=%async_computation.3 | async-start | bytes 4194304 | tf_op jit(solution)/shard_map/all_to_all | solution.py:19
  220.6 0.2 copy.62
  220.9 0.1 reshape_squeeze.7
  221.0 26.0 %all-to-all-done.3 = bf16[2,1024,4,128]{3,1,0,2:T(8,128)(2,1)S(1)} async-done(((bf16[2,1024,4,128]{3,1,0,2:T(8,128)(2,1)}), bf16[2,1024,4,128]{3,1,0,2:T(8,128)(2,1)S(1)}, u32[]{:S(2)}, u32[]{:S(2)}) %all-to-all-start.3) | async-done | bytes 2097184 | tf_op jit(solution)/shard_map/all_to_all | solution.py:19
  247.0 2.9 fusion.16
  249.9 2.2 copy.64
  252.0 29.5 %all_to_all.57 = bf16[2,1024,512]{2,0,1:T(2,128)(2,1)S(1)} all-to-all(bf16[2,1024,512]{2,0,1:T(2,128)(2,1)S(1)} %copy.64), channel_id=1, replica_groups=mesh['seq'=64,'chan'=4] {'chan'}, dimensions={1} | all-to-all | bytes 4194304 | tf_op jit(solution)/shard_map/all_to_all | solution.py:60
  281.5 2.9 %copy.65 = bf16[2,256,4,512]{3,2,1,0:T(4,128)(2,1)} copy(bf16[2,256,4,512]{3,0,1,2:T(2,128)(2,1)S(1)} %bitcast.58) | data formatting | bytes 4194304 | tf_op jit(solution)/shard_map/all_to_all | solution.py:60
  284.5 4.4 %all_to_all.49 = bf16[2,256,2048]{2,1,0:T(8,128)(2,1)} reshape(bf16[2,256,4,512]{3,2,1,0:T(4,128)(2,1)} %copy.65) | data formatting | bytes 4194304 | tf_op jit(solution)/shard_map/all_to_all | solution.py:60
  (14 shorter events, 0.0 us)
Async XLA Ops:
  0.0 196.9 %copy-start = (bf16[1,512,2048]{2,1,0:T(8,128)(2,1)S(1)}, bf16[1,512,2048]{2,1,0:T(8,128)(2,1)}, u32[]{:S(2)}) copy-start(bf16[1,512,2048]{2,1,0:T(8,128)(2,1)} %param.16) | copy-start | bytes 6291460
  74.3 1.3 copy-start.3
  146.5 5.4 %copy-start.5 = (f32[512]{0:T(512)S(1)}, f32[512]{0:T(512)}, u32[]{:S(2)}) copy-start(f32[512]{0:T(512)} %param.13) | copy-start | bytes 6148
  146.5 5.4 %copy-start.6 = (f32[512]{0:T(512)S(1)}, f32[512]{0:T(512)}, u32[]{:S(2)}) copy-start(f32[512]{0:T(512)} %param.12) | copy-start | bytes 6148
  151.9 4.3 %copy-start.7 = (bf16[1,512,512]{2,1,0:T(8,128)(2,1)S(1)}, bf16[1,512,512]{2,1,0:T(8,128)(2,1)}, u32[]{:S(2)}) copy-start(bf16[1,512,512]{2,1,0:T(8,128)(2,1)} %param.14) | copy-start | bytes 1572868
  156.2 2.6 copy-start.2
  162.8 34.1 %all-to-all-start.2 = ((bf16[2,1024,4,128]{3,1,0,2:T(8,128)(2,1)}), bf16[2,1024,4,128]{3,1,0,2:T(8,128)(2,1)}, u32[]{:S(2)}, u32[]{:S(2)}) async-start(bf16[2,1024,4,128]{3,1,0,2:T(8,128)(2,1)} %copy.58), calls=%async_computation.2 | async-start | bytes 4194304 | tf_op jit(solution)/shard_map/all_to_all | solution.py:19
  216.1 4.6 %copy-start.4 = (bf16[1,512,512]{2,1,0:T(8,128)(2,1)S(1)}, bf16[1,512,512]{2,1,0:T(8,128)(2,1)}, u32[]{:S(2)}) copy-start(bf16[1,512,512]{2,1,0:T(8,128)(2,1)} %param.17) | copy-start | bytes 1572868
  216.1 30.9 %all-to-all-start.3 = ((bf16[2,1024,4,128]{3,1,0,2:T(8,128)(2,1)}), bf16[2,1024,4,128]{3,1,0,2:T(8,128)(2,1)S(1)}, u32[]{:S(2)}, u32[]{:S(2)}) async-start(bf16[2,1024,4,128]{3,1,0,2:T(8,128)(2,1)} %copy.61), calls=%async_computation.3 | async-start | bytes 4194304 | tf_op jit(solution)/shard_map/all_to_all | solution.py:19
  281.5 7.4 %copy-start.1 = (bf16[1,512,2048]{2,1,0:T(8,128)(2,1)S(1)}, bf16[1,512,2048]{2,1,0:T(8,128)(2,1)}, u32[]{:S(2)}) copy-start(bf16[1,512,2048]{2,1,0:T(8,128)(2,1)} %param.16) | copy-start | bytes 6291460
where the time goes:
time: 290 us; the launch traced here: 289 us
  blocking collectives  149 us (51%)
  local copies, waits for them, and re-layouts  51.3 us (18%)
  waiting for transfers between devices  44.4 us (15%)
  matrix products  27.1 us (9%)
  starting transfers between devices  12.3 us (4%)
  other arithmetic  4.97 us (2%)
    all_to_all x1, blocking collectives, on_device(): lax.all_to_all(first_pass, 'seq', split_axis=2, concat_axis=1, tiled=True)  63.2 us
    all_to_all x1, blocking collectives, on_device(): lax.all_to_all(mixed_rows, 'seq', split_axis=1, concat_axis=2, tiled=True)  56.1 us
    all_to_all x2, waiting for transfers between devices, shard_monarch(): lax.all_to_all(inner_rows, 'chan', split_axis=2, concat_axis=2, tiled=True)  44.4 us
    all_to_all x1, blocking collectives, on_device(): lax.all_to_all(result, 'chan', split_axis=1, concat_axis=2, tiled=True)  29.5 us
    dot_general x2, matrix products, shard_monarch(): jnp.einsum('qp,stp->stq', inner_weight[0], values, preferred_element_type...  17.8 us
    all_to_all x2, starting transfers between devices, shard_monarch(): lax.all_to_all(inner_rows, 'chan', split_axis=2, concat_axis=2, tiled=True)  12.3 us
    convert_element_type x3, local copies, waits for them, and re-layouts, on_device(): restored.astype(jnp.float32)  10.9 us
    reshape x2, local copies, waits for them, and re-layouts, shard_monarch(): inner_rows.astype(jnp.bfloat16)  7.9 us
  transfers between devices with their start and end apart: 2, of which 2 were waited for; matrix products, arithmetic and copies ran while one was open for 3% of the time, Pallas kernels for 0%

commit v1 on v0

v1 whole, which is shorter than its diff:
```python
import functools

import jax
import jax.numpy as jnp
from jax import lax
from jax.experimental import pallas as pl
from jax.experimental.pallas import tpu as pltpu
from jax.sharding import PartitionSpec as P

BF16 = jnp.bfloat16
F32 = jnp.float32
BOTH = ("seq", "chan")
MIB = 1 << 20
VMEM = pl.BlockSpec(memory_space=pltpu.VMEM)
HBM = pl.BlockSpec(memory_space=pl.ANY)


def params(mib):
    return pltpu.CompilerParams(vmem_limit_bytes=mib * MIB)


def mm(a, b):
    return jnp.dot(a, b, preferred_element_type=F32)


def mm_nt(a, b):
    return lax.dot_general(a, b, (((1,), (1,)), ((), ())), preferred_element_type=F32)


def iota2(shape, axis):
    return lax.broadcasted_iota(jnp.int32, shape, axis)


def one_hot(shape, pick):
    return jnp.where(pick(iota2(shape, 0), iota2(shape, 1)), 1.0, 0.0).astype(BF16)


def first_kernel(x_ref, m_ref, o_ref, acc):
    for a in range(4):
        for s in range(2):
            acc[:, s * 4 + a, :] = mm(m_ref[a], x_ref[s, a])
    o_ref[...] = acc[...].reshape(64, 32, 512).astype(BF16)


def first_mix(x, m):
    return pl.pallas_call(
        first_kernel,
        out_shape=jax.ShapeDtypeStruct((64, 32, 512), BF16),
        in_specs=[VMEM, VMEM],
        out_specs=VMEM,
        scratch_shapes=[pltpu.VMEM((256, 8, 512), F32)],
        compiler_params=params(32),
        cost_estimate=pl.CostEstimate(flops=2**29, bytes_accessed=5 * MIB, transcendentals=0),
        name="first_mix",
    )(x, m)


def spread_kernel(m_ref, o_ref):
    rows = one_hot((256, 256), lambda r, x: x == (r % 64) * 4 + r // 64)
    for b in range(4):
        turned = mm(rows, m_ref[b]).astype(BF16)
        for s in range(2):
            slot = (b % 2) * 2 + s
            place = one_hot(
                (256, 1024),
                lambda y, k: k == (y // 4) * 16 + (b % 2) * 8 + s * 4 + y % 4,
            )
            o_ref[b // 2, slot * 256 : (slot + 1) * 256, :] = mm(turned, place).astype(BF16)


def spread(m):
    return pl.pallas_call(
        spread_kernel,
        out_shape=jax.ShapeDtypeStruct((2, 1024, 1024), BF16),
        in_specs=[VMEM],
        out_specs=VMEM,
        compiler_params=params(32),
        cost_estimate=pl.CostEstimate(flops=2**30, bytes_accessed=5 * MIB, transcendentals=0),
        name="spread",
    )(m)


def second_kernel(r_ref, m_ref, o_ref, acc):
    for p in range(2):
        part = r_ref[:, p * 16 : (p + 1) * 16, :].reshape(1024, 512)
        for slot in range(4):
            b, s = p * 2 + slot // 2, slot % 2
            acc[:, s * 4 + b, :] = mm(m_ref[p, slot * 256 : (slot + 1) * 256, :], part)
    o_ref[...] = acc[...].astype(BF16)


def second_mix(received, m):
    return pl.pallas_call(
        second_kernel,
        out_shape=jax.ShapeDtypeStruct((256, 8, 512), BF16),
        in_specs=[VMEM, VMEM],
        out_specs=VMEM,
        scratch_shapes=[pltpu.VMEM((256, 8, 512), F32)],
        compiler_params=params(32),
        cost_estimate=pl.CostEstimate(flops=2**31, bytes_accessed=8 * MIB, transcendentals=0),
        name="second_mix",
    )(received, m)


def pack_kernel(w1, w2, w3, w4, o_ref):
    same = one_hot((512, 512), lambda r, c: r == c)
    turn = one_hot((512, 512), lambda k, m: m == (k % 128) * 4 + k // 128)
    o_ref[0:512, :] = mm_nt(same, w1[0]).astype(BF16)
    for j in range(4):
        lo = 512 + j * 512
        o_ref[lo : lo + 512, :] = mm_nt(turn, w2[0, j * 512 : (j + 1) * 512, :]).astype(BF16)
        lo = 2560 + j * 512
        o_ref[lo : lo + 512, :] = mm_nt(same, w3[0, :, j * 512 : (j + 1) * 512]).astype(BF16)
    o_ref[4608:5120, :] = mm_nt(turn, w4[0]).astype(BF16)


def pack(w1, w2, w3, w4):
    return pl.pallas_call(
        pack_kernel,
        out_shape=jax.ShapeDtypeStruct((5120, 512), BF16),
        in_specs=[VMEM] * 4,
        out_specs=VMEM,
        compiler_params=params(32),
        cost_estimate=pl.CostEstimate(flops=2**31, bytes_accessed=10 * MIB, transcendentals=0),
        name="pack",
    )(w1, w2, w3, w4)


def mlp_kernel(
    meta, r_hbm, x0, x1, x2, x3, gs_ref, gb_ref, w_own, w_core,
    n0, n1, n2, n3, c0, c1, c2, c3, o_ref,
    rec, xin, wts, hid, mid, mid2, rec_sem, x_sem, w_sem,
):
    chan, y = meta[0], meta[1]
    copies = [pltpu.make_async_copy(r_hbm, rec, rec_sem)]
    for k, src in enumerate((x0, x1, x2, x3)):
        copies.append(pltpu.make_async_copy(src, xin.at[chan ^ k], x_sem.at[k]))
    weights = [
        pltpu.make_async_copy(w_own, wts.at[chan], w_sem.at[0]),
        pltpu.make_async_copy(w_core, wts.at[chan ^ 1], w_sem.at[1]),
    ]
    for flip, pieces in ((2, (n0, n1, n2, n3)), (3, (c0, c1, c2, c3))):
        for src, off in zip(pieces, (0, 3, 1, 2)):
            lo = pl.multiple_of(((y + off) % 4) * 1280, 1280)
            sem = w_sem.at[len(weights)]
            weights.append(
                pltpu.make_async_copy(src, wts.at[chan ^ flip, pl.ds(lo, 1280), :], sem)
            )
    for c in copies + weights:
        c.start()
    for c in copies:
        c.wait()
    order = one_hot(
        (512, 512),
        lambda r, k: k == ((r % 256) // 4) * 8 + (r // 256) * 4 + r % 4,
    )
    for c in range(4):
        lanes = slice(c * 512, (c + 1) * 512)
        mixed = mm(order, rec[c])
        res = xin[c].reshape(512, 512).astype(F32)
        z = gs_ref[0:1, lanes] * res + gb_ref[0:1, lanes]
        hid[:, lanes] = (res + mixed * (0.5 * jnp.tanh(0.5 * z) + 0.5)).astype(BF16)
    for c in weights:
        c.wait()
    for c in range(4):
        inner = mm(hid[:, c * 512 : (c + 1) * 512], wts[c, 0:512, :]).astype(BF16)
        for l in range(4):
            mid[l, :, c * 128 : (c + 1) * 128] = inner[:, l * 128 : (l + 1) * 128]
    for l in range(4):
        total = None
        for j in range(4):
            e = mm(mid[l], wts[l, 512 + j * 512 : 1024 + j * 512, :])
            u = e * (0.7978845608028654 + 0.035677408136300125 * (e * e))
            half = 0.5 * e
            act = (half + half * jnp.tanh(u)).astype(BF16)
            t = mm(act, wts[l, 2560 + j * 512 : 3072 + j * 512, :])
            total = t if total is None else total + t
        inner = total.astype(BF16)
        for k in range(4):
            mid2[k, :, l * 128 : (l + 1) * 128] = inner[:, k * 128 : (k + 1) * 128]
    for k in range(4):
        lanes = slice(k * 512, (k + 1) * 512)
        t = mm(mid2[k], wts[k, 4608:5120, :])
        o_ref[:, :, lanes] = (hid[:, lanes].astype(F32) + t).astype(BF16).reshape(2, 256, 512)


def mlp(meta, received, xs, gs, gb, w_own, w_core, near, cross):
    smem = pl.BlockSpec(memory_space=pltpu.SMEM)
    return pl.pallas_call(
        mlp_kernel,
        out_shape=jax.ShapeDtypeStruct((2, 256, 2048), BF16),
        in_specs=[smem] + [HBM] * 5 + [VMEM] * 2 + [HBM] * 10,
        out_specs=VMEM,
        scratch_shapes=[
            pltpu.VMEM((4, 512, 512), BF16),
            pltpu.VMEM((4, 2, 256, 512), BF16),
            pltpu.VMEM((4, 5120, 512), BF16),
            pltpu.VMEM((512, 2048), BF16),
            pltpu.VMEM((4, 512, 512), BF16),
            pltpu.VMEM((4, 512, 512), BF16),
            pltpu.SemaphoreType.DMA,
            pltpu.SemaphoreType.DMA((4,)),
            pltpu.SemaphoreType.DMA((10,)),
        ],
        compiler_params=params(52),
        cost_estimate=pl.CostEstimate(
            flops=11 * 2**30, bytes_accessed=26 * MIB, transcendentals=5 * MIB
        ),
        name="mlp",
    )(meta, received, *xs, gs, gb, w_own, w_core, *near, *cross)


def place(y, z, xl, h, c):
    return (((y % 4) * 8 + z) * 2 + xl) * 4 + h * 2 + c


def pairs(move):
    out = []
    for i in range(256):
        seq, chan = divmod(i, 4)
        y, rest = divmod(seq, 16)
        z, xl = divmod(rest, 2)
        out.append((i, place(*move(y, z, xl, chan // 2, chan % 2))))
    return out


def next_along_x(y, z, xl, h, c):
    return y, z, 1 - xl, 1 - h, c


TO_X = pairs(next_along_x)
TO_CORE = pairs(lambda y, z, xl, h, c: (y, z, xl, h, 1 - c))
TO_CHAN = [
    pairs(lambda y, z, xl, h, c, k=k: (y, z, xl, h ^ (k >> 1), c ^ (k & 1))) for k in range(4)
]


def along_y(step):
    return pairs(lambda y, z, xl, h, c: (y + step, z, xl, h, c))


def on_device(
    inputs, mix_first, mix_second, gate_scale, gate_bias, up_first, up_second, down_first, down_second
):
    chan = lax.axis_index("chan")
    y = lax.axis_index("seq") // 16
    meta = jnp.stack([chan, y]).astype(jnp.int32)
    grouped = inputs.reshape(2, 4, 256, 512)
    sent = first_mix(grouped, mix_first)
    received = lax.all_to_all(sent, "seq", split_axis=0, concat_axis=0, tiled=True)

    sent, up_first, mix_second = lax.optimization_barrier((sent, up_first, mix_second))
    spread_second = spread(mix_second)
    packed = pack(up_first, up_second, down_first, down_second)
    gates = lax.all_gather(jnp.stack([gate_scale, gate_bias]), "chan", axis=1, tiled=True)
    xs = []
    for k in range(4):
        part = lax.dynamic_index_in_dim(grouped, chan ^ k, 1, keepdims=False)
        xs.append(lax.ppermute(part, BOTH, TO_CHAN[k]) if k else part)
    quarter = lax.dynamic_slice_in_dim(packed, y * 1280, 1280, 0)
    near = [lax.ppermute(quarter, BOTH, TO_X)]
    near += [lax.ppermute(near[0], BOTH, along_y(step)) for step in (1, -1, 2)]
    w_core = lax.ppermute(packed, BOTH, TO_CORE)
    cross = [lax.ppermute(piece, BOTH, TO_CORE) for piece in near]

    sent2 = second_mix(received, spread_second)
    received2 = lax.all_to_all(sent2, ("chan", "seq"), split_axis=0, concat_axis=0, tiled=True)
    return mlp(
        meta, received2.reshape(4, 512, 512), xs, gates[0:1], gates[1:2], packed, w_core, near, cross
    )


def solution(mesh):
    return jax.shard_map(
        on_device,
        mesh=mesh,
        in_specs=(
            P(None, "seq", "chan"),
            P("seq", None, None),
            P("seq", None, None),
            P("chan"),
            P("chan"),
            P("chan", None, None),
            P("chan", None, None),
            P("chan", None, None),
            P("chan", None, None),
        ),
        out_specs=P(None, ("seq", "chan"), None),
        check_vma=False,
    )
```

time: 290 us -> 247 us (0.85)
  blocking collectives: 149 us -> 7.11 us
  waiting for transfers between devices: 44.4 us -> 139 us
  Pallas kernels: 0 us -> 38.9 us
  local copies, waits for them, and re-layouts: 51.3 us -> 16.7 us
  starting transfers between devices: 12.3 us -> 44.3 us
  matrix products: 27.1 us -> 0 us
  other arithmetic: 4.97 us -> 0.08 us
    all_to_all x3 -> x0, blocking collectives: 149 us -> none  [the longest x1 63.2 us: on_device(): lax.all_to_all(first_pass, 'seq', split_axis=2, concat_axis=1, tiled=True)]
    ppermute x0 -> x12, waiting for transfers between devices: none -> 104 us  [the longest x1 56.2 us: on_device(): near = [lax.ppermute(quarter, BOTH, TO_X)]]
    pallas_call x0 -> x5, Pallas kernels: none -> 38.9 us  [the longest x1 23.9 us: mlp(): pl.pallas_call(mlp_kernel, out_shape=jax.ShapeDtypeStruct((2, 256, 2048),...]
    dot_general x5 -> x0, matrix products: 27.1 us -> none  [the longest x2 17.8 us: shard_monarch(): jnp.einsum('qp,stp->stq', inner_weight[0], values, preferred_element_type...]
    convert_element_type x6 -> x0, local copies, waits for them, and re-layouts: 25.5 us -> none  [the longest x3 10.9 us: on_device(): restored.astype(jnp.float32)]
    ppermute x0 -> x12, starting transfers between devices: none -> 19.5 us  [the longest x3 5.53 us: on_device(): near += [lax.ppermute(near[0], BOTH, along_y(step)) for step in (1, -1, 2)]]
    all_to_all x2, starting transfers between devices: 12.3 us -> 24.8 us  [the longest x1 13.7 us: on_device(): lax.all_to_all(sent, 'seq', split_axis=0, concat_axis=0, tiled=True)]
    unnamed x18 -> x40, local copies, waits for them, and re-layouts: 4.21 us -> 14 us
  transfers between devices with their start and end apart: 2 -> 14, of which waited for: 2 -> 6; matrix products, arithmetic and copies ran while one was open for 3% -> 1% of each run, Pallas kernels for 0% -> 5%
where the time goes in v1:
time: 247 us
  waiting for transfers between devices  139 us (56%)
  starting transfers between devices  44.3 us (18%)
  Pallas kernels  38.9 us (16%)
  local copies, waits for them, and re-layouts  16.7 us (7%)
  blocking collectives  7.11 us (3%)
    ppermute x1, waiting for transfers between devices, on_device(): near = [lax.ppermute(quarter, BOTH, TO_X)]  56.2 us
    all_to_all x1, waiting for transfers between devices, on_device(): lax.all_to_all(sent, 'seq', split_axis=0, concat_axis=0, tiled=True)  35.1 us
    ppermute x3, waiting for transfers between devices, on_device(): near += [lax.ppermute(near[0], BOTH, along_y(step)) for step in (1, -1, 2)]  34.6 us
    pallas_call x1, Pallas kernels, mlp(): pl.pallas_call(mlp_kernel, out_shape=jax.ShapeDtypeStruct((2, 256, 2048),...  23.9 us
    unnamed x40, local copies, waits for them, and re-layouts  14 us
    all_to_all x1, starting transfers between devices, on_device(): lax.all_to_all(sent, 'seq', split_axis=0, concat_axis=0, tiled=True)  13.7 us
    ppermute x3, waiting for transfers between devices, on_device(): xs.append(lax.ppermute(part, BOTH, TO_CHAN[k]) if k else part)  13.5 us
    all_to_all x1, starting transfers between devices, on_device(): lax.all_to_all(sent2, ('chan', 'seq'), split_axis=0, concat_axis=0, tiled...  11.1 us
  transfers between devices with their start and end apart: 14, of which 6 were waited for; matrix products, arithmetic and copies ran while one was open for 1% of the time, Pallas kernels for 5%

profile of v1, /device:TPU:1, one launch (start us, length us, event | category | flops | bytes accessed | tf_op | source)
XLA Modules:
  0.0 247.0 jit_solution(11551920101738954671)
XLA Ops:
  0.0 1.6 copy-done.2
  1.6 1.0 copy-done.6
  2.6 3.0 %first_mix.1 = bf16[64,32,512]{2,1,0:T(8,128)(2,1)} custom-call(bf16[2,4,256,512]{3,2,1,0:T(8,128)(2,1)S(1)} %bitcast.14, bf16[4,256,256]{2,1,0:T(8,128)(2,1)S(1)} %copy-done.6), custom_call_target="tpu_custom_call" | custom-call | flops 536870912 | bytes 5242880 | tf_op jit(solution)/shard_map/first_mix/pallas_call | solution.py:46
  5.7 13.7 %all-to-all-start = ((bf16[64,32,512]{2,1,0:T(8,128)(2,1)}), bf16[64,32,512]{2,1,0:T(8,128)(2,1)S(1)}, u32[]{:S(2)}, u32[]{:S(2)}) async-start(bf16[64,32,512]{2,1,0:T(8,128)(2,1)} %first_mix.1), calls=%async_computation | async-start | bytes 4194304 | tf_op jit(solution)/shard_map/all_to_all | solution.py:250
  19.4 1.6 copy-done.4
  21.0 1.6 copy-done.5
  22.6 5.2 %pack.1.w_own = bf16[5120,512]{1,0:T(8,128)(2,1)} custom-call(bf16[1,512,512]{2,1,0:T(8,128)(2,1)S(1)} %copy-done.7, bf16[1,2048,512]{2,1,0:T(8,128)(2,1)S(1)} %copy-done.4, bf16[1,512,2048]{2,1,0:T(8,128)(2,1)S(1)} %copy-done.5, bf16[1,512,512]{2,1,0:T(8,128)(2,1)S(1)} %copy-done.8), custom_call_target="tpu_custom_call" | custom-call | flops 2147483648 | bytes 10485760 | tf_op jit(solution)/shard_map/pack/pallas_call | solution.py:118
  27.8 1.0 collective-permute-start.3
  28.8 1.0 copy-done.9
  29.8 2.0 spread.1.m_ref
  31.9 2.0 copy-done
  33.9 35.1 %all-to-all-done.r_ref = bf16[64,32,512]{2,1,0:T(8,128)(2,1)S(1)} async-done(((bf16[64,32,512]{2,1,0:T(8,128)(2,1)}), bf16[64,32,512]{2,1,0:T(8,128)(2,1)S(1)}, u32[]{:S(2)}, u32[]{:S(2)}) %all-to-all-start) | async-done | bytes 2097184 | tf_op jit(solution)/shard_map/all_to_all | solution.py:250
  69.0 2.2 copy-done.1
  71.2 4.7 %second_mix.1 = bf16[256,8,512]{2,1,0:T(8,128)(2,1)} custom-call(bf16[64,32,512]{2,1,0:T(8,128)(2,1)S(1)} %all-to-all-done.r_ref, bf16[2,1024,1024]{2,1,0:T(8,128)(2,1)S(1)} %copy-done.1), custom_call_target="tpu_custom_call" | custom-call | flops 2147483648 | bytes 8388608 | tf_op jit(solution)/shard_map/second_mix/pallas_call | solution.py:93
  75.9 11.1 %all-to-all-start.1 = ((bf16[256,8,512]{2,1,0:T(8,128)(2,1)}), bf16[256,8,512]{2,1,0:T(8,128)(2,1)}, u32[]{:S(2)}, u32[]{:S(2)}) async-start(bf16[256,8,512]{2,1,0:T(8,128)(2,1)} %second_mix.1), calls=%async_computation.1 | async-start | bytes 4194304 | tf_op jit(solution)/shard_map/all_to_all | solution.py:267
  87.0 2.6 %constant_dynamic-slice_fusion = bf16[1280,512]{1,0:T(8,128)(2,1)} fusion(bf16[5120,512]{1,0:T(8,128)(2,1)} %pack.1.w_own, s32[]{:T(128)S(6)} %select_n.26), kind=kLoop, calls=%fused_computation.5 | loop fusion | bytes 2621444 | tf_op jit(solution)/shard_map/dynamic_slice | solution.py:260
  89.6 2.6 %collective-permute-start.4 = (bf16[1280,512]{1,0:T(8,128)(2,1)}, bf16[1280,512]{1,0:T(8,128)(2,1)}, u32[]{:S(2)}, u32[]{:S(2)}) collective-permute-start(bf16[1280,512]{1,0:T(8,128)(2,1)} %constant_dynamic-slice_fusion), channel_id=1, source_target_pairs={{0,6},{1,7},{2,4},{3,5},{4,2},{5,3},{6,0},{7,1},{8,14},{9,15},{10,... | collective-permute-start | bytes 3932168 | tf_op jit(solution)/shard_map/ppermute | solution.py:261
  92.4 1.4 collective-permute-start.2
  93.7 56.2 %collective-permute-done.4.n0 = bf16[1280,512]{1,0:T(8,128)(2,1)} collective-permute-done((bf16[1280,512]{1,0:T(8,128)(2,1)}, bf16[1280,512]{1,0:T(8,128)(2,1)}, u32[]{:S(2)}, u32[]{:S(2)}) %collective-permute-start.4) | collective-permute-done | bytes 1310752 | tf_op jit(solution)/shard_map/ppermute | solution.py:261
  150.0 4.1 %collective-permute-start.7 = (bf16[1280,512]{1,0:T(8,128)(2,1)}, bf16[1280,512]{1,0:T(8,128)(2,1)S(1)}, u32[]{:S(2)}, u32[]{:S(2)}) collective-permute-start(bf16[1280,512]{1,0:T(8,128)(2,1)} %collective-permute-done.4.n0), channel_id=1, source_target_pairs={{0,128},{1,129},{2,130},{3,131},{4,132},{5,133},{6,134},{7,135},{8... | collective-permute-start | bytes 3932168 | tf_op jit(solution)/shard_map/ppermute | solution.py:262
  155.5 1.2 collective-permute-start.1
  156.7 12.0 %collective-permute-done.1.x2 = bf16[2,256,512]{2,1,0:T(8,128)(2,1)S(1)} collective-permute-done((bf16[2,256,512]{2,1,0:T(8,128)(2,1)S(1)}, bf16[2,256,512]{2,1,0:T(8,128)(2,1)S(1)}, u32[]{:S(2)}, u32[]{:S(2)}) %collective-permute-start.1) | collective-permute-done | bytes 524320 | tf_op jit(solution)/shard_map/ppermute | solution.py:259
  168.7 2.7 %collective-permute-start = (bf16[2,256,512]{2,1,0:T(8,128)(2,1)S(1)}, bf16[2,256,512]{2,1,0:T(8,128)(2,1)S(1)}, u32[]{:S(2)}, u32[]{:S(2)}) collective-permute-start(bf16[2,256,512]{2,1,0:T(8,128)(2,1)S(1)} %get-tuple-element.11), channel_id=1, source_target_pairs={{0,1},{1,0},{2,3},{3,2},{4,5},{5,4},{6,7},{7,6},{8,9},{9,8},{10,11... | collective-permute-start | bytes 1572872 | tf_op jit(solution)/shard_map/ppermute | solution.py:259
  171.4 1.5 collective-permute-done.x1
  173.3 8.9 %collective-permute-done.7.n3 = bf16[1280,512]{1,0:T(8,128)(2,1)S(1)} collective-permute-done((bf16[1280,512]{1,0:T(8,128)(2,1)}, bf16[1280,512]{1,0:T(8,128)(2,1)S(1)}, u32[]{:S(2)}, u32[]{:S(2)}) %collective-permute-start.7) | collective-permute-done | bytes 1310752 | tf_op jit(solution)/shard_map/ppermute | solution.py:262
  182.2 3.3 %collective-permute-start.11 = (bf16[1280,512]{1,0:T(8,128)(2,1)S(1)}, bf16[1280,512]{1,0:T(8,128)(2,1)S(1)}, u32[]{:S(2)}, u32[]{:S(2)}) collective-permute-start(bf16[1280,512]{1,0:T(8,128)(2,1)S(1)} %collective-permute-done.7.n3), channel_id=1, source_target_pairs={{0,1},{1,0},{2,3},{3,2},{4,5},{5,4},{6,7},{7,6},{8,9},{9,8},{10,11... | collective-permute-start | bytes 3932168 | tf_op jit(solution)/shard_map/ppermute | solution.py:264
  185.5 25.7 %collective-permute-done.6.n2 = bf16[1280,512]{1,0:T(8,128)(2,1)S(1)} collective-permute-done((bf16[1280,512]{1,0:T(8,128)(2,1)}, bf16[1280,512]{1,0:T(8,128)(2,1)S(1)}, u32[]{:S(2)}, u32[]{:S(2)}) %collective-permute-start.6) | collective-permute-done | bytes 1310752 | tf_op jit(solution)/shard_map/ppermute | solution.py:262
  211.2 1.4 collective-permute-start.10
  212.7 7.1 %all_gather.3 = f32[2,2048]{1,0:T(2,128)S(1)} all-gather(f32[2,512]{1,0:T(2,128)S(1)} %pad_maximum_fusion), channel_id=1, replica_groups=mesh['seq'=64,'chan'=4] {'chan'}, dimensions={1}, use_global_device_ids=true | all-gather | bytes 20480 | tf_op jit(solution)/shard_map/all_gather | solution.py:255
  220.0 1.0 copy-done.15
  221.8 1.1 copy-done.18
  222.9 23.9 %mlp.1 = bf16[2,256,2048]{2,1,0:T(8,128)(2,1)} custom-call(s32[2]{0:T(128)S(1)} %pad_add_fusion.meta, bf16[4,512,512]{2,1,0:T(8,128)(2,1)} %bitcast.3.r_hbm, bf16[2,256,512]{2,1,0:T(8,128)(2,1)S(1)} %get-tuple-element.12.x0, bf16[2,256,512]{2,1,0:T(8,128)(2,1)S(1)} %collective-permute-done.x1, bf16[2,256,512]{2,1,0:T(8,128)(2,1)S(1)} %collective-permute-done.1.x2, ...), custom_call_target="tpu_custom_call" | custom-call | flops 11811160064 | bytes 27262976 | tf_op jit(solution)/shard_map/mlp/pallas_call | solution.py:189
  (47 shorter events, 3.1 us)
Async XLA Ops:
  0.0 1.6 copy-start.2
  5.7 13.7 %copy-start.7 = (bf16[1,512,512]{2,1,0:T(8,128)(2,1)S(1)}, bf16[1,512,512]{2,1,0:T(8,128)(2,1)}, u32[]{:S(2)}) copy-start(bf16[1,512,512]{2,1,0:T(8,128)(2,1)} %w1) | copy-start | bytes 1572868
  5.7 13.7 %copy-start.8 = (bf16[1,512,512]{2,1,0:T(8,128)(2,1)S(1)}, bf16[1,512,512]{2,1,0:T(8,128)(2,1)}, u32[]{:S(2)}) copy-start(bf16[1,512,512]{2,1,0:T(8,128)(2,1)} %w4.1) | copy-start | bytes 1572868
  5.7 63.3 %all-to-all-start = ((bf16[64,32,512]{2,1,0:T(8,128)(2,1)}), bf16[64,32,512]{2,1,0:T(8,128)(2,1)S(1)}, u32[]{:S(2)}, u32[]{:S(2)}) async-start(bf16[64,32,512]{2,1,0:T(8,128)(2,1)} %first_mix.1), calls=%async_computation | async-start | bytes 4194304 | tf_op jit(solution)/shard_map/all_to_all | solution.py:250
  19.4 1.6 copy-start.4
  21.0 1.6 copy-start.5
  27.8 195.0 %collective-permute-start.3 = (bf16[5120,512]{1,0:T(8,128)(2,1)}, bf16[5120,512]{1,0:T(8,128)(2,1)}, u32[]{:S(2)}, u32[]{:S(2)}) collective-permute-start(bf16[5120,512]{1,0:T(8,128)(2,1)} %pack.1.w_own), channel_id=1, source_target_pairs={{0,1},{1,0},{2,3},{3,2},{4,5},{5,4},{6,7},{7,6},{8,9},{9,8},{10,11... | collective-permute-start | bytes 15728648 | tf_op jit(solution)/shard_map/ppermute | solution.py:263
  31.9 2.1 copy-start
  69.0 2.2 copy-start.1
  75.9 147.0 %all-to-all-start.1 = ((bf16[256,8,512]{2,1,0:T(8,128)(2,1)}), bf16[256,8,512]{2,1,0:T(8,128)(2,1)}, u32[]{:S(2)}, u32[]{:S(2)}) async-start(bf16[256,8,512]{2,1,0:T(8,128)(2,1)} %second_mix.1), calls=%async_computation.1 | async-start | bytes 4194304 | tf_op jit(solution)/shard_map/all_to_all | solution.py:267
  87.0 5.2 %copy-start.3 = (bf16[2,1024,512]{2,1,0:T(8,128)(2,1)S(1)}, bf16[2,1024,512]{2,1,0:T(8,128)(2,1)}, u32[]{:S(2)}) copy-start(bf16[2,1024,512]{2,1,0:T(8,128)(2,1)} %param.9) | copy-start | bytes 6291460
  89.6 60.4 %collective-permute-start.4 = (bf16[1280,512]{1,0:T(8,128)(2,1)}, bf16[1280,512]{1,0:T(8,128)(2,1)}, u32[]{:S(2)}, u32[]{:S(2)}) collective-permute-start(bf16[1280,512]{1,0:T(8,128)(2,1)} %constant_dynamic-slice_fusion), channel_id=1, source_target_pairs={{0,6},{1,7},{2,4},{3,5},{4,2},{5,3},{6,0},{7,1},{8,14},{9,15},{10,... | collective-permute-start | bytes 3932168 | tf_op jit(solution)/shard_map/ppermute | solution.py:261
  92.2 120.5 %copy-start.10 = (f32[512]{0:T(512)S(1)}, f32[512]{0:T(512)}, u32[]{:S(2)}) copy-start(f32[512]{0:T(512)} %param.13) | copy-start | bytes 6148
  92.2 120.5 %copy-start.11 = (f32[512]{0:T(512)S(1)}, f32[512]{0:T(512)}, u32[]{:S(2)}) copy-start(f32[512]{0:T(512)} %param.12) | copy-start | bytes 6148
  92.4 63.2 %collective-permute-start.2 = (bf16[2,256,512]{2,1,0:T(8,128)(2,1)S(1)}, bf16[2,256,512]{2,1,0:T(8,128)(2,1)S(1)}, u32[]{:S(2)}, u32[]{:S(2)}) collective-permute-start(bf16[2,256,512]{2,1,0:T(8,128)(2,1)S(1)} %get-tuple-element.9), channel_id=1, source_target_pairs={{0,3},{1,2},{2,1},{3,0},{4,7},{5,6},{6,5},{7,4},{8,11},{9,10},{10,... | collective-permute-start | bytes 1572872 | tf_op jit(solution)/shard_map/ppermute | solution.py:259
  150.0 32.2 %collective-permute-start.7 = (bf16[1280,512]{1,0:T(8,128)(2,1)}, bf16[1280,512]{1,0:T(8,128)(2,1)S(1)}, u32[]{:S(2)}, u32[]{:S(2)}) collective-permute-start(bf16[1280,512]{1,0:T(8,128)(2,1)} %collective-permute-done.4.n0), channel_id=1, source_target_pairs={{0,128},{1,129},{2,130},{3,131},{4,132},{5,133},{6,134},{7,135},{8... | collective-permute-start | bytes 3932168 | tf_op jit(solution)/shard_map/ppermute | solution.py:262
  154.0 57.1 %collective-permute-start.6 = (bf16[1280,512]{1,0:T(8,128)(2,1)}, bf16[1280,512]{1,0:T(8,128)(2,1)S(1)}, u32[]{:S(2)}, u32[]{:S(2)}) collective-permute-start(bf16[1280,512]{1,0:T(8,128)(2,1)} %collective-permute-done.4.n0), channel_id=1, source_target_pairs={{0,192},{1,193},{2,194},{3,195},{4,196},{5,197},{6,198},{7,199},{8... | collective-permute-start | bytes 3932168 | tf_op jit(solution)/shard_map/ppermute | solution.py:262
  154.9 57.7 %collective-permute-start.5 = (bf16[1280,512]{1,0:T(8,128)(2,1)}, bf16[1280,512]{1,0:T(8,128)(2,1)S(1)}, u32[]{:S(2)}, u32[]{:S(2)}) collective-permute-start(bf16[1280,512]{1,0:T(8,128)(2,1)} %collective-permute-done.4.n0), channel_id=1, source_target_pairs={{0,64},{1,65},{2,66},{3,67},{4,68},{5,69},{6,70},{7,71},{8,72},{9,... | collective-permute-start | bytes 3932168 | tf_op jit(solution)/shard_map/ppermute | solution.py:262
  155.5 67.4 %copy-start.19 = (bf16[2,256,512]{2,1,0:T(8,128)(2,1)}, bf16[2,256,512]{2,1,0:T(8,128)(2,1)S(1)}, u32[]{:S(2)}) copy-start(bf16[2,256,512]{2,1,0:T(8,128)(2,1)S(1)} %collective-permute-done.2.x3) | copy-start | bytes 1572868
  155.5 13.2 %collective-permute-start.1 = (bf16[2,256,512]{2,1,0:T(8,128)(2,1)S(1)}, bf16[2,256,512]{2,1,0:T(8,128)(2,1)S(1)}, u32[]{:S(2)}, u32[]{:S(2)}) collective-permute-start(bf16[2,256,512]{2,1,0:T(8,128)(2,1)S(1)} %get-tuple-element.10), channel_id=1, source_target_pairs={{0,2},{1,3},{2,0},{3,1},{4,6},{5,7},{6,4},{7,5},{8,10},{9,11},{10,... | collective-permute-start | bytes 1572872 | tf_op jit(solution)/shard_map/ppermute | solution.py:259
  168.7 4.2 %collective-permute-start = (bf16[2,256,512]{2,1,0:T(8,128)(2,1)S(1)}, bf16[2,256,512]{2,1,0:T(8,128)(2,1)S(1)}, u32[]{:S(2)}, u32[]{:S(2)}) collective-permute-start(bf16[2,256,512]{2,1,0:T(8,128)(2,1)S(1)} %get-tuple-element.11), channel_id=1, source_target_pairs={{0,1},{1,0},{2,3},{3,2},{4,5},{5,4},{6,7},{7,6},{8,9},{9,8},{10,11... | collective-permute-start | bytes 1572872 | tf_op jit(solution)/shard_map/ppermute | solution.py:259
  172.9 47.1 %collective-permute-start.8 = (bf16[1280,512]{1,0:T(8,128)(2,1)}, bf16[1280,512]{1,0:T(8,128)(2,1)S(1)}, u32[]{:S(2)}, u32[]{:S(2)}) collective-permute-start(bf16[1280,512]{1,0:T(8,128)(2,1)} %collective-permute-done.4.n0), channel_id=1, source_target_pairs={{0,1},{1,0},{2,3},{3,2},{4,5},{5,4},{6,7},{7,6},{8,9},{9,8},{10,11... | collective-permute-start | bytes 3932168 | tf_op jit(solution)/shard_map/ppermute | solution.py:264
  182.2 37.8 %copy-start.12 = (bf16[1280,512]{1,0:T(8,128)(2,1)}, bf16[1280,512]{1,0:T(8,128)(2,1)S(1)}, u32[]{:S(2)}) copy-start(bf16[1280,512]{1,0:T(8,128)(2,1)S(1)} %collective-permute-done.7.n3) | copy-start | bytes 3932164
  182.2 37.8 %collective-permute-start.11 = (bf16[1280,512]{1,0:T(8,128)(2,1)S(1)}, bf16[1280,512]{1,0:T(8,128)(2,1)S(1)}, u32[]{:S(2)}, u32[]{:S(2)}) collective-permute-start(bf16[1280,512]{1,0:T(8,128)(2,1)S(1)} %collective-permute-done.7.n3), channel_id=1, source_target_pairs={{0,1},{1,0},{2,3},{3,2},{4,5},{5,4},{6,7},{7,6},{8,9},{9,8},{10,11... | collective-permute-start | bytes 3932168 | tf_op jit(solution)/shard_map/ppermute | solution.py:264
  211.2 8.8 %copy-start.13 = (bf16[1280,512]{1,0:T(8,128)(2,1)}, bf16[1280,512]{1,0:T(8,128)(2,1)S(1)}, u32[]{:S(2)}) copy-start(bf16[1280,512]{1,0:T(8,128)(2,1)S(1)} %collective-permute-done.6.n2) | copy-start | bytes 3932164
  211.2 8.8 %collective-permute-start.10 = (bf16[1280,512]{1,0:T(8,128)(2,1)S(1)}, bf16[1280,512]{1,0:T(8,128)(2,1)S(1)}, u32[]{:S(2)}, u32[]{:S(2)}) collective-permute-start(bf16[1280,512]{1,0:T(8,128)(2,1)S(1)} %collective-permute-done.6.n2), channel_id=1, source_target_pairs={{0,1},{1,0},{2,3},{3,2},{4,5},{5,4},{6,7},{7,6},{8,9},{9,8},{10,11... | collective-permute-start | bytes 3932168 | tf_op jit(solution)/shard_map/ppermute | solution.py:264
  212.6 7.4 %copy-start.14 = (bf16[1280,512]{1,0:T(8,128)(2,1)}, bf16[1280,512]{1,0:T(8,128)(2,1)S(1)}, u32[]{:S(2)}) copy-start(bf16[1280,512]{1,0:T(8,128)(2,1)S(1)} %collective-permute-done.5.n1) | copy-start | bytes 3932164
  212.6 7.4 %collective-permute-start.9 = (bf16[1280,512]{1,0:T(8,128)(2,1)S(1)}, bf16[1280,512]{1,0:T(8,128)(2,1)S(1)}, u32[]{:S(2)}, u32[]{:S(2)}) collective-permute-start(bf16[1280,512]{1,0:T(8,128)(2,1)S(1)} %collective-permute-done.5.n1), channel_id=1, source_target_pairs={{0,1},{1,0},{2,3},{3,2},{4,5},{5,4},{6,7},{7,6},{8,9},{9,8},{10,11... | collective-permute-start | bytes 3932168 | tf_op jit(solution)/shard_map/ppermute | solution.py:264
  220.0 1.1 copy-start.15
  220.0 1.5 copy-start.16
  220.0 1.8 copy-start.17
  221.8 1.1 copy-start.18
  (2 other events, 2.1 us)

commit v2 on v1

v2 whole, which is shorter than its diff:
```python
import functools

import jax
import jax.numpy as jnp
from jax import lax
from jax.experimental import pallas as pl
from jax.experimental.pallas import tpu as pltpu
from jax.sharding import PartitionSpec as P

BF16 = jnp.bfloat16
F32 = jnp.float32
BOTH = ("seq", "chan")
MIB = 1 << 20
FULL = 58
CUT = 256
VMEM = pl.BlockSpec(memory_space=pltpu.VMEM)
HBM = pl.BlockSpec(memory_space=pltpu.HBM)
SMEM = pl.BlockSpec(memory_space=pltpu.SMEM)


def params(mib):
    return pltpu.CompilerParams(vmem_limit_bytes=mib * MIB)


def mm(a, b):
    return jnp.dot(a, b, preferred_element_type=F32)


def mm_nt(a, b):
    return lax.dot_general(a, b, (((1,), (1,)), ((), ())), preferred_element_type=F32)


def iota2(shape, axis):
    return lax.broadcasted_iota(jnp.int32, shape, axis)


def one_hot(shape, pick):
    return jnp.where(pick(iota2(shape, 0), iota2(shape, 1)), 1.0, 0.0).astype(BF16)


def first_kernel(lo, hi, meta, x_hbm, m_hbm, o_ref, acc, x, m, sems):
    copies = []
    for a in range(4):
        copies.append(
            (
                pltpu.make_async_copy(m_hbm.at[a], m.at[a], sems.at[2 * a]),
                pltpu.make_async_copy(x_hbm.at[:, a, :, lo:hi], x.at[a], sems.at[2 * a + 1]),
            )
        )
    for pair in copies:
        for c in pair:
            c.start()
    for a in range(4):
        for c in copies[a]:
            c.wait()
        for s in range(2):
            acc[:, s * 4 + a, :] = mm(m[a], x[a, s])
    o_ref[...] = acc[...].reshape(64, 32, hi - lo).astype(BF16)


def first_mix(lo, hi, meta, x, m):
    lanes = hi - lo
    return pl.pallas_call(
        functools.partial(first_kernel, lo, hi),
        out_shape=jax.ShapeDtypeStruct((64, 32, lanes), BF16),
        in_specs=[SMEM, HBM, HBM],
        out_specs=VMEM,
        scratch_shapes=[
            pltpu.VMEM((256, 8, lanes), F32),
            pltpu.VMEM((4, 2, 256, lanes), BF16),
            pltpu.VMEM((4, 256, 256), BF16),
            pltpu.SemaphoreType.DMA((8,)),
        ],
        compiler_params=params(FULL),
        cost_estimate=pl.CostEstimate(flops=2**29, bytes_accessed=5 * MIB, transcendentals=0),
        name=f"first_mix_{lo}",
    )(meta, x, m)


def spread_kernel(meta, m_ref, o_ref):
    rows = one_hot((256, 256), lambda r, x: x == (r % 64) * 4 + r // 64)
    for b in range(4):
        turned = mm(rows, m_ref[b]).astype(BF16)
        for s in range(2):
            slot = (b % 2) * 2 + s
            place = one_hot(
                (256, 1024),
                lambda y, k: k == (y // 4) * 16 + (b % 2) * 8 + s * 4 + y % 4,
            )
            o_ref[b // 2, slot * 256 : (slot + 1) * 256, :] = mm(turned, place).astype(BF16)


def spread(meta, m):
    return pl.pallas_call(
        spread_kernel,
        out_shape=jax.ShapeDtypeStruct((2, 1024, 1024), BF16),
        in_specs=[SMEM, VMEM],
        out_specs=VMEM,
        compiler_params=params(FULL),
        cost_estimate=pl.CostEstimate(flops=2**30, bytes_accessed=5 * MIB, transcendentals=0),
        name="spread",
    )(meta, m)


def second_kernel(lo, hi, r_hbm, m_hbm, *refs):
    *before, o_ref, acc, r, m, sems = refs
    copies = []
    for p in range(2):
        rows = pl.ds(p * 16, 16)
        copies.append(pltpu.make_async_copy(r_hbm.at[:, rows, :], r.at[p], sems.at[2 * p]))
        copies.append(pltpu.make_async_copy(m_hbm.at[p], m.at[p], sems.at[2 * p + 1]))
    if before:
        copies.append(pltpu.make_async_copy(before[0], o_ref.at[:, :, 0:lo], sems.at[4]))
    for c in copies:
        c.start()
    for p in range(2):
        copies[2 * p].wait()
        copies[2 * p + 1].wait()
        part = r[p].reshape(1024, hi - lo)
        for slot in range(4):
            b, s = p * 2 + slot // 2, slot % 2
            acc[:, s * 4 + b, :] = mm(m[p, slot * 256 : (slot + 1) * 256, :], part)
    if before:
        copies[4].wait()
        o_ref[:, :, lo:hi] = acc[...].astype(BF16)
    else:
        o_ref[...] = acc[...].astype(BF16)


def second_mix(lo, hi, received, m, *before):
    lanes = hi - lo
    return pl.pallas_call(
        functools.partial(second_kernel, lo, hi),
        out_shape=jax.ShapeDtypeStruct((256, 8, hi if before else lanes), BF16),
        in_specs=[HBM] * (2 + len(before)),
        out_specs=VMEM,
        scratch_shapes=[
            pltpu.VMEM((256, 8, lanes), F32),
            pltpu.VMEM((2, 64, 16, lanes), BF16),
            pltpu.VMEM((2, 1024, 1024), BF16),
            pltpu.SemaphoreType.DMA((5,)),
        ],
        compiler_params=params(FULL),
        cost_estimate=pl.CostEstimate(flops=2**30, bytes_accessed=6 * MIB, transcendentals=0),
        name=f"second_mix_{lo}",
    )(received, m, *before)


A_ROWS, B_ROWS = 656, 640


def same_rows(n, first):
    return one_hot((n, 512), lambda r, c: c == r + first)


def turned_rows(n, first):
    return one_hot((n, 512), lambda r, m: m == ((r + first) % 128) * 4 + (r + first) // 128)


def gate_rows(g_ref):
    rows = []
    for v in range(2):
        rest = g_ref[v : v + 1, :]
        for _ in range(3):
            part = rest.astype(BF16).astype(F32)
            rows.append(part)
            rest = rest - part
    return jnp.concatenate(rows + [jnp.zeros((10, 512), F32)], axis=0).astype(BF16)


def quarter_kernel(meta, g_ref, w1, w2, w3, w4, a_ref, b_ref, v1, v2, v3, v4, sem):
    y = meta[1]
    lo = pl.multiple_of(y * 512, 512)
    copies = [
        pltpu.make_async_copy(w1.at[0], v1, sem.at[0]),
        pltpu.make_async_copy(w2.at[0, pl.ds(lo, 512), :], v2, sem.at[1]),
        pltpu.make_async_copy(w3.at[0, :, pl.ds(lo, 512)], v3, sem.at[2]),
        pltpu.make_async_copy(w4.at[0], v4, sem.at[3]),
    ]
    for c in copies:
        c.start()
    for c in copies:
        c.wait()
    a_ref[0:128, :] = mm_nt(same_rows(128, y * 128), v1[...]).astype(BF16)
    a_ref[128:640, :] = mm_nt(turned_rows(512, 0), v2[...]).astype(BF16)
    a_ref[640:656, :] = gate_rows(g_ref)
    b_ref[0:512, :] = mm_nt(same_rows(512, 0), v3[...]).astype(BF16)
    b_ref[512:640, :] = mm_nt(turned_rows(128, y * 128), v4[...]).astype(BF16)


def quarter(meta, gate, w1, w2, w3, w4):
    return pl.pallas_call(
        quarter_kernel,
        out_shape=(
            jax.ShapeDtypeStruct((A_ROWS, 512), BF16),
            jax.ShapeDtypeStruct((B_ROWS, 512), BF16),
        ),
        in_specs=[SMEM, VMEM] + [HBM] * 4,
        out_specs=(VMEM, VMEM),
        scratch_shapes=[pltpu.VMEM((512, 512), BF16)] * 4 + [pltpu.SemaphoreType.DMA((4,))],
        compiler_params=params(FULL),
        cost_estimate=pl.CostEstimate(flops=2**29, bytes_accessed=4 * MIB, transcendentals=0),
        name="quarter",
    )(meta, gate, w1, w2, w3, w4)


def pack_kernel(meta, g_ref, w1, w2, w3, w4, o_ref):
    same = same_rows(512, 0)
    turn = turned_rows(512, 0)
    first = mm_nt(same, w1[0]).astype(BF16)
    last = mm_nt(turn, w4[0]).astype(BF16)
    for j in range(4):
        wide = slice(j * 512, (j + 1) * 512)
        o_ref[j, 0:128, :] = first[j * 128 : (j + 1) * 128]
        o_ref[j, 128:640, :] = mm_nt(turn, w2[0, wide, :]).astype(BF16)
        o_ref[j, 640:656, :] = gate_rows(g_ref)
        o_ref[j, 656:1168, :] = mm_nt(same, w3[0, :, wide]).astype(BF16)
        o_ref[j, 1168:1296, :] = last[j * 128 : (j + 1) * 128]


def pack(meta, gate, w1, w2, w3, w4):
    return pl.pallas_call(
        pack_kernel,
        out_shape=jax.ShapeDtypeStruct((4, A_ROWS + B_ROWS, 512), BF16),
        in_specs=[SMEM] + [VMEM] * 5,
        out_specs=VMEM,
        compiler_params=params(FULL),
        cost_estimate=pl.CostEstimate(flops=2**31, bytes_accessed=10 * MIB, transcendentals=0),
        name="pack",
    )(meta, gate, w1, w2, w3, w4)


def mlp_kernel(
    meta, r_hbm, x0, x1, x2, x3, own, swapped, near_a, near_b, cross_a, cross_b,
    o_ref, rec, xin, gate, hid, mid, mid2, w1, w2, w3, w4, sems,
):
    chan = meta[0]
    waits = {}
    count = [0]

    def fetch(key, src, dst):
        copy = pltpu.make_async_copy(src, dst, sems.at[count[0]])
        count[0] += 1
        copy.start()
        waits.setdefault(key, []).append(copy)

    spans = ((0, 128), (128, 640), (640, 656), (656, 1168), (1168, 1296))

    def fetch_part(part, k):
        dst = (w1, w2, gate, w3, w4)[part]
        lo, hi = spans[part]
        block = chan ^ k
        if k < 2:
            src = (own, swapped)[k]
            if part == 2:
                fetch((part, k), src.at[0, lo:hi, :], dst.at[block])
            else:
                fetch((part, k), src.at[:, lo:hi, :], dst.at[block])
        else:
            first, last = (near_a, near_b) if k == 2 else (cross_a, cross_b)
            src, base = (first, 0) if part < 3 else (last, A_ROWS)
            if part == 2:
                fetch((part, k), src.at[0, lo - base : hi - base, :], dst.at[block])
            else:
                fetch((part, k), src.at[:, lo - base : hi - base, :], dst.at[block])

    def ready(part, k):
        for copy in waits[(part, k)]:
            copy.wait()

    for k, x_ref in enumerate((x0, x1, x2, x3)):
        fetch((5, k), r_hbm.at[chan ^ k], rec.at[k])
        fetch((5, k), x_ref, xin.at[k])
        fetch_part(2, k)
        fetch_part(0, k)
    for k in range(4):
        fetch_part(1, k)
        fetch_part(3, k)
    for k in range(4):
        fetch_part(4, k)

    order = one_hot(
        (512, 512),
        lambda r, k: k == ((r % 256) // 4) * 8 + (r // 256) * 4 + r % 4,
    )
    for k in range(4):
        c = chan ^ k
        ready(5, k)
        mixed = mm(order, rec[k])
        res = xin[k].reshape(512, 512).astype(F32)
        ready(2, k)
        g = gate[c].astype(F32)
        scale = (g[0:1] + g[1:2]) + g[2:3]
        bias = (g[3:4] + g[4:5]) + g[5:6]
        z = scale * res + bias
        hidden = (res + mixed * (0.5 * jnp.tanh(0.5 * z) + 0.5)).astype(BF16)
        hid[c] = hidden
        ready(0, k)
        inner = mm(hidden, w1[c].reshape(512, 512)).astype(BF16)
        for l in range(4):
            mid[l, c] = inner[:, l * 128 : (l + 1) * 128]
    for k in range(4):
        l = chan ^ k
        rows = jnp.concatenate([mid[l, c] for c in range(4)], axis=1)
        ready(1, k)
        ready(3, k)
        total = None
        for j in range(4):
            e = mm(rows, w2[l, j])
            u = e * (0.7978845608028654 + 0.035677408136300125 * (e * e))
            half = 0.5 * e
            act = (half + half * jnp.tanh(u)).astype(BF16)
            t = mm(act, w3[l, j])
            total = t if total is None else total + t
        inner = total.astype(BF16)
        for n in range(4):
            mid2[n, l] = inner[:, n * 128 : (n + 1) * 128]
    for k in range(4):
        n = chan ^ k
        rows = jnp.concatenate([mid2[n, l] for l in range(4)], axis=1)
        ready(4, k)
        t = mm(rows, w4[n].reshape(512, 512))
        out = (hid[n].astype(F32) + t).astype(BF16)
        o_ref[:, :, pl.ds(pl.multiple_of(n * 512, 512), 512)] = out.reshape(2, 256, 512)


def mlp(meta, received, xs, own, swapped, near, cross):
    wide = pltpu.VMEM((4, 4, 512, 512), BF16)
    narrow = pltpu.VMEM((4, 4, 128, 512), BF16)
    tall = pltpu.VMEM((4, 4, 512, 128), BF16)
    return pl.pallas_call(
        mlp_kernel,
        out_shape=jax.ShapeDtypeStruct((2, 256, 2048), BF16),
        in_specs=[SMEM] + [HBM] * 11,
        out_specs=VMEM,
        scratch_shapes=[
            pltpu.VMEM((4, 512, 512), BF16),
            pltpu.VMEM((4, 2, 256, 512), BF16),
            pltpu.VMEM((4, 16, 512), BF16),
            pltpu.VMEM((4, 512, 512), BF16),
            tall,
            tall,
            narrow,
            wide,
            wide,
            narrow,
            pltpu.SemaphoreType.DMA((28,)),
        ],
        compiler_params=params(FULL),
        cost_estimate=pl.CostEstimate(
            flops=11 * 2**30, bytes_accessed=26 * MIB, transcendentals=5 * MIB
        ),
        name="mlp",
    )(meta, received, *xs, own, swapped, *near, *cross)


def place(y, z, xl, h, c):
    return (((y % 4) * 8 + z) * 2 + xl) * 4 + h * 2 + c


def pairs(move):
    out = []
    for i in range(256):
        seq, chan = divmod(i, 4)
        y, rest = divmod(seq, 16)
        z, xl = divmod(rest, 2)
        out.append((i, place(*move(y, z, xl, chan // 2, chan % 2))))
    return out


def next_along_x(y, z, xl, h, c):
    return y, z, 1 - xl, 1 - h, c


TO_X = pairs(next_along_x)
TO_CORE = pairs(lambda y, z, xl, h, c: (y, z, xl, h, 1 - c))
TO_CHAN = [
    pairs(lambda y, z, xl, h, c, k=k: (y, z, xl, h ^ (k >> 1), c ^ (k & 1))) for k in range(4)
]


RINGS = [[y * 16 + rest for y in range(4)] for rest in range(16)]


def gather_ring(piece):
    out = lax.all_gather(piece, "seq", axis_index_groups=RINGS, axis=0, tiled=True)
    return out.reshape(4, *piece.shape)


def on_device(
    inputs, mix_first, mix_second, gate_scale, gate_bias, up_first, up_second, down_first, down_second
):
    bar = lax.optimization_barrier
    chan = lax.axis_index("chan")
    y = lax.axis_index("seq") // 16
    meta = jnp.stack([chan, y]).astype(jnp.int32)
    gate = jnp.stack([gate_scale, gate_bias])
    grouped = inputs.reshape(2, 4, 256, 512)
    to_b = lambda sent: lax.all_to_all(sent, "seq", split_axis=0, concat_axis=0, tiled=True)
    move = lambda piece, to: lax.ppermute(piece, BOTH, to)

    sent0 = first_mix(0, CUT, meta, grouped, mix_first)
    received0 = to_b(sent0)
    _, meta = bar((sent0, meta))
    mine_a, mine_b = quarter(meta, gate, up_first, up_second, down_first, down_second)
    near_a, near_b = move(mine_a, TO_X), move(mine_b, TO_X)
    _, meta = bar((mine_a, meta))
    sent1 = first_mix(CUT, 512, meta, grouped, mix_first)
    received0, near_a, sent1, meta = bar((received0, near_a, sent1, meta))
    received1 = to_b(sent1)
    near_a = gather_ring(near_a)
    spread_second = spread(meta, mix_second)
    own = pack(meta, gate, up_first, up_second, down_first, down_second)
    turned0 = second_mix(0, CUT, received0, spread_second)
    received1, spread_second, turned0, near_b, own, meta = bar(
        (received1, spread_second, turned0, near_b, own, meta)
    )
    near_b = gather_ring(near_b)
    turned = second_mix(CUT, 512, received1, spread_second, turned0)
    back = lax.all_to_all(turned, ("chan", "seq"), split_axis=0, concat_axis=0, tiled=True)
    _, own, meta = bar((turned, own, meta))
    xs = []
    for k in range(4):
        part = lax.dynamic_index_in_dim(grouped, meta[0] ^ k, 1, keepdims=False)
        xs.append(move(part, TO_CHAN[k]) if k else part)
    swapped, cross_a = move(own, TO_CORE), move(near_a, TO_CORE)
    near_b, xs, swapped, cross_a = bar((near_b, xs, swapped, cross_a))
    near, cross = [near_a, near_b], [cross_a, move(near_b, TO_CORE)]
    return mlp(meta, back.reshape(4, 512, 512), xs, own, swapped, near, cross)


def solution(mesh):
    return jax.shard_map(
        on_device,
        mesh=mesh,
        in_specs=(
            P(None, "seq", "chan"),
            P("seq", None, None),
            P("seq", None, None),
            P("chan"),
            P("chan"),
            P("chan", None, None),
            P("chan", None, None),
            P("chan", None, None),
            P("chan", None, None),
        ),
        out_specs=P(None, ("seq", "chan"), None),
        check_vma=False,
    )
```

time: 247 us -> 194 us (0.79)
  waiting for transfers between devices: 139 us -> 70.3 us
  Pallas kernels: 38.9 us -> 57 us
  between operations: 0.37 us -> 13.8 us
  local copies, waits for them, and re-layouts: 16.7 us -> 4.28 us
  blocking collectives: 7.11 us -> 0 us
    ppermute x12 -> x8, waiting for transfers between devices: 104 us -> 53.4 us  [on_device(): move = lambda piece, to: lax.ppermute(piece, BOTH, to)]
    all_to_all x1 -> x2, waiting for transfers between devices: 35.1 us -> 11.5 us  [on_device(): lax.all_to_all(sent, 'seq', split_axis=0, concat_axis=0, tiled=True)]
    pallas_call x3 -> x6, Pallas kernels: 13 us -> 30.3 us  [the longest x2 9.86 us: second_mix(): pl.pallas_call(functools.partial(second_kernel, lo, hi), out_shape=jax.Sh...]
    unnamed x40 -> x24, local copies, waits for them, and re-layouts: 14 us -> 3.35 us
    all_to_all x1 -> x2, starting transfers between devices: 13.7 us -> 21.1 us  [on_device(): lax.all_to_all(sent, 'seq', split_axis=0, concat_axis=0, tiled=True)]
    all_gather x1 -> x0, blocking collectives: 7.11 us -> none  [on_device(): lax.all_gather(jnp.stack([gate_scale, gate_bias]), 'chan', axis=1, tiled=...]
    ppermute x12 -> x8, starting transfers between devices: 19.5 us -> 14 us  [on_device(): move = lambda piece, to: lax.ppermute(piece, BOTH, to)]
    pallas_call x1, Pallas kernels: 2.01 us -> 5.13 us  [spread(): pl.pallas_call(spread_kernel, out_shape=jax.ShapeDtypeStruct((2, 1024, 10...]
  transfers between devices with their start and end apart: 14 -> 13, of which waited for: 6 -> 8; matrix products, arithmetic and copies ran while one was open for 1% -> 1% of each run, Pallas kernels for 5% -> 16%
where the time goes in v2:
time: 194 us; the launch traced here: 193 us
  waiting for transfers between devices  70.3 us (36%)
  Pallas kernels  57 us (29%)
  starting transfers between devices  46.5 us (24%)
  between operations  13.8 us (7%)
  local copies, waits for them, and re-layouts  4.28 us (2%)
    ppermute x8, waiting for transfers between devices, on_device(): move = lambda piece, to: lax.ppermute(piece, BOTH, to)  53.4 us
    pallas_call x1, Pallas kernels, mlp(): pl.pallas_call(mlp_kernel, out_shape=jax.ShapeDtypeStruct((2, 256, 2048),...  21.6 us
    all_to_all x2, starting transfers between devices, on_device(): lax.all_to_all(sent, 'seq', split_axis=0, concat_axis=0, tiled=True)  21.1 us
    ppermute x8, starting transfers between devices, on_device(): move = lambda piece, to: lax.ppermute(piece, BOTH, to)  14 us
    all_to_all x2, waiting for transfers between devices, on_device(): lax.all_to_all(sent, 'seq', split_axis=0, concat_axis=0, tiled=True)  11.5 us
    all_to_all x1, starting transfers between devices, on_device(): lax.all_to_all(turned, ('chan', 'seq'), split_axis=0, concat_axis=0, tile...  11.4 us
    pallas_call x2, Pallas kernels, second_mix(): pl.pallas_call(functools.partial(second_kernel, lo, hi), out_shape=jax.Sh...  9.86 us
    pallas_call x2, Pallas kernels, first_mix(): pl.pallas_call(functools.partial(first_kernel, lo, hi), out_shape=jax.Sha...  8.38 us
  transfers between devices with their start and end apart: 13, of which 8 were waited for; matrix products, arithmetic and copies ran while one was open for 1% of the time, Pallas kernels for 16%

profile of v2, /device:TPU:1, one launch (start us, length us, event | category | flops | bytes accessed | tf_op | source)
XLA Modules:
  0.0 193.1 jit_solution(3266558026412421767)
XLA Ops:
  6.5 0.6 pad_add_fusion.meta
  7.1 4.3 %first_mix_0.1 = bf16[64,32,256]{2,1,0:T(8,128)(2,1)} custom-call(s32[2]{0:T(128)} %pad_add_fusion.meta, bf16[2,4,256,512]{3,2,1,0:T(8,128)(2,1)} %bitcast.18, bf16[4,256,256]{2,1,0:T(8,128)(2,1)} %m_hbm.3), custom_call_target="tpu_custom_call" | custom-call | flops 536870912 | bytes 5242880 | tf_op jit(solution)/shard_map/first_mix_0/pallas_call | solution.py:63
  11.4 13.6 %all-to-all-start = ((bf16[64,32,256]{2,1,0:T(8,128)(2,1)}), bf16[64,32,256]{2,1,0:T(8,128)(2,1)S(1)}, u32[]{:S(2)}, u32[]{:S(2)}) async-start(bf16[64,32,256]{2,1,0:T(8,128)(2,1)} %first_mix_0.1), calls=%async_computation | async-start | bytes 2097152 | tf_op jit(solution)/shard_map/all_to_all | solution.py:399
  25.1 0.6 pad_maximum_fusion.g_ref
  25.7 4.3 %quarter.1 = (bf16[656,512]{1,0:T(8,128)(2,1)}, bf16[640,512]{1,0:T(8,128)(2,1)}) custom-call(s32[2]{0:T(128)} %pad_add_fusion.meta, f32[2,512]{1,0:T(2,128)} %pad_maximum_fusion.g_ref, bf16[1,512,512]{2,1,0:T(8,128)(2,1)} %w1.3, bf16[1,2048,512]{2,1,0:T(8,128)(2,1)} %w2.3, bf16[1,512,2048]{2,1,0:T(8,128)(2,1)} %w3.3, bf16[1,512,512]{2,1,0:T(8,128)(2,1)} %w4.3), custom_call_target="tpu_custom_call" | custom-call | flops 536870912 | bytes 4194304 | tf_op jit(solution)/shard_map/quarter/pallas_call | solution.py:192
  30.0 2.4 %collective-permute-start = (bf16[656,512]{1,0:T(8,128)(2,1)}, bf16[656,512]{1,0:T(8,128)(2,1)S(1)}, u32[]{:S(2)}, u32[]{:S(2)}) collective-permute-start(bf16[656,512]{1,0:T(8,128)(2,1)} %get-tuple-element.29), channel_id=1, source_target_pairs={{0,6},{1,7},{2,4},{3,5},{4,2},{5,3},{6,0},{7,1},{8,14},{9,15},{10,... | collective-permute-start | bytes 2015240 | tf_op jit(solution)/shard_map/ppermute | solution.py:400
  32.3 4.1 %first_mix_256.1 = bf16[64,32,256]{2,1,0:T(8,128)(2,1)} custom-call(s32[2]{0:T(128)} %pad_add_fusion.meta, bf16[2,4,256,512]{3,2,1,0:T(8,128)(2,1)} %bitcast.19, bf16[4,256,256]{2,1,0:T(8,128)(2,1)} %m_hbm.3), custom_call_target="tpu_custom_call" | custom-call | flops 536870912 | bytes 5242880 | tf_op jit(solution)/shard_map/first_mix_256/pallas_call | solution.py:63
  36.5 10.6 %collective-permute-done = bf16[656,512]{1,0:T(8,128)(2,1)S(1)} collective-permute-done((bf16[656,512]{1,0:T(8,128)(2,1)}, bf16[656,512]{1,0:T(8,128)(2,1)S(1)}, u32[]{:S(2)}, u32[]{:S(2)}) %collective-permute-start) | collective-permute-done | bytes 671776 | tf_op jit(solution)/shard_map/ppermute | solution.py:400
  47.1 5.0 %all-to-all-done.r_hbm = bf16[64,32,256]{2,1,0:T(8,128)(2,1)S(1)} async-done(((bf16[64,32,256]{2,1,0:T(8,128)(2,1)}), bf16[64,32,256]{2,1,0:T(8,128)(2,1)S(1)}, u32[]{:S(2)}, u32[]{:S(2)}) %all-to-all-start) | async-done | bytes 1048608 | tf_op jit(solution)/shard_map/all_to_all | solution.py:399
  52.1 7.5 %all-to-all-start.1 = ((bf16[64,32,256]{2,1,0:T(8,128)(2,1)}), bf16[64,32,256]{2,1,0:T(8,128)(2,1)S(1)}, u32[]{:S(2)}, u32[]{:S(2)}) async-start(bf16[64,32,256]{2,1,0:T(8,128)(2,1)} %first_mix_256.1), calls=%async_computation.1 | async-start | bytes 2097152 | tf_op jit(solution)/shard_map/all_to_all | solution.py:399
  59.6 2.5 %collective-permute-start.1 = (bf16[640,512]{1,0:T(8,128)(2,1)S(1)}, bf16[640,512]{1,0:T(8,128)(2,1)S(1)}, u32[]{:S(2)}, u32[]{:S(2)}) collective-permute-start(bf16[640,512]{1,0:T(8,128)(2,1)S(1)} %copy-done.9), channel_id=1, source_target_pairs={{0,6},{1,7},{2,4},{3,5},{4,2},{5,3},{6,0},{7,1},{8,14},{9,15},{10,... | collective-permute-start | bytes 1966088 | tf_op jit(solution)/shard_map/ppermute | solution.py:400
  62.2 5.1 %spread.1.m_hbm = bf16[2,1024,1024]{2,1,0:T(8,128)(2,1)} custom-call(s32[2]{0:T(128)} %pad_add_fusion.meta, bf16[4,256,256]{2,1,0:T(8,128)(2,1)} %m_ref.1), custom_call_target="tpu_custom_call" | custom-call | flops 1073741824 | bytes 5242880 | tf_op jit(solution)/shard_map/spread/pallas_call | solution.py:94
  67.3 4.8 %second_mix_0.1.refs_0_ = bf16[256,8,256]{2,1,0:T(8,128)(2,1)} custom-call(bf16[64,32,256]{2,1,0:T(8,128)(2,1)} %copy-done.1, bf16[2,1024,1024]{2,1,0:T(8,128)(2,1)} %spread.1.m_hbm), custom_call_target="tpu_custom_call" | custom-call | flops 1073741824 | bytes 6291456 | tf_op jit(solution)/shard_map/second_mix_0/pallas_call | solution.py:132
  72.1 7.8 %pack.1.own = bf16[4,1296,512]{2,1,0:T(8,128)(2,1)} custom-call(s32[2]{0:T(128)} %pad_add_fusion.meta, f32[2,512]{1,0:T(2,128)} %pad_maximum_fusion.g_ref, bf16[1,512,512]{2,1,0:T(8,128)(2,1)} %w1.3, bf16[1,2048,512]{2,1,0:T(8,128)(2,1)} %w2.3, bf16[1,512,2048]{2,1,0:T(8,128)(2,1)} %w3.3, bf16[1,512,512]{2,1,0:T(8,128)(2,1)} %w4.3), custom_call_target="tpu_custom_call" | custom-call | flops 2147483648 | bytes 10485760 | tf_op jit(solution)/shard_map/pack/pallas_call | solution.py:222
  79.8 6.5 %all-to-all-done.1.r_hbm = bf16[64,32,256]{2,1,0:T(8,128)(2,1)S(1)} async-done(((bf16[64,32,256]{2,1,0:T(8,128)(2,1)}), bf16[64,32,256]{2,1,0:T(8,128)(2,1)S(1)}, u32[]{:S(2)}, u32[]{:S(2)}) %all-to-all-start.1) | async-done | bytes 1048608 | tf_op jit(solution)/shard_map/all_to_all | solution.py:399
  86.4 1.0 copy-done.2
  87.3 5.1 %second_mix_256.1 = bf16[256,8,512]{2,1,0:T(8,128)(2,1)} custom-call(bf16[64,32,256]{2,1,0:T(8,128)(2,1)} %copy-done.2, bf16[2,1024,1024]{2,1,0:T(8,128)(2,1)} %spread.1.m_hbm, bf16[256,8,256]{2,1,0:T(8,128)(2,1)} %second_mix_0.1.refs_0_), custom_call_target="tpu_custom_call" | custom-call | flops 1073741824 | bytes 6291456 | tf_op jit(solution)/shard_map/second_mix_256/pallas_call | solution.py:132
  92.5 3.1 %collective-permute-start.5 = (bf16[4,1296,512]{2,1,0:T(8,128)(2,1)}, bf16[4,1296,512]{2,1,0:T(8,128)(2,1)}, u32[]{:S(2)}, u32[]{:S(2)}) collective-permute-start(bf16[4,1296,512]{2,1,0:T(8,128)(2,1)} %pack.1.own), channel_id=1, source_target_pairs={{0,1},{1,0},{2,3},{3,2},{4,5},{5,4},{6,7},{7,6},{8,9},{9,8},{10,11... | collective-permute-start | bytes 15925256 | tf_op jit(solution)/shard_map/ppermute | solution.py:400
  95.6 2.8 %all-gather.5.cloned.1.call-done = bf16[2624,512]{1,0:T(8,128)(2,1)} async-done(((bf16[656,512]{1,0:T(8,128)(2,1)}), bf16[2624,512]{1,0:T(8,128)(2,1)}) %all-gather.5.cloned.1.call-update) | async-done | bytes 2686992 | tf_op jit(solution)/shard_map/all_gather | solution.py:386
  98.4 0.6 collective-permute-start.6
  99.0 11.4 %all-to-all-start.2 = ((bf16[256,8,512]{2,1,0:T(8,128)(2,1)}), bf16[256,8,512]{2,1,0:T(8,128)(2,1)}, u32[]{:S(2)}, u32[]{:S(2)}) async-start(bf16[256,8,512]{2,1,0:T(8,128)(2,1)} %second_mix_256.1), calls=%async_computation.2 | async-start | bytes 4194304 | tf_op jit(solution)/shard_map/all_to_all | solution.py:420
  110.6 0.9 dynamic-slice_bitcast_fusion
  111.6 3.1 %collective-permute-start.4 = (bf16[2,256,512]{2,1,0:T(8,128)(2,1)S(1)}, bf16[2,256,512]{2,1,0:T(8,128)(2,1)S(1)}, u32[]{:S(2)}, u32[]{:S(2)}) collective-permute-start(bf16[2,256,512]{2,1,0:T(8,128)(2,1)S(1)} %get-tuple-element.51), channel_id=1, source_target_pairs={{0,3},{1,2},{2,1},{3,0},{4,7},{5,6},{6,5},{7,4},{8,11},{9,10},{10,... | collective-permute-start | bytes 1572872 | tf_op jit(solution)/shard_map/ppermute | solution.py:400
  114.7 1.9 %collective-permute-start.3 = (bf16[2,256,512]{2,1,0:T(8,128)(2,1)S(1)}, bf16[2,256,512]{2,1,0:T(8,128)(2,1)S(1)}, u32[]{:S(2)}, u32[]{:S(2)}) collective-permute-start(bf16[2,256,512]{2,1,0:T(8,128)(2,1)S(1)} %get-tuple-element.52), channel_id=1, source_target_pairs={{0,2},{1,3},{2,0},{3,1},{4,6},{5,7},{6,4},{7,5},{8,10},{9,11},{10,... | collective-permute-start | bytes 1572872 | tf_op jit(solution)/shard_map/ppermute | solution.py:400
  116.7 18.9 %collective-permute-done.4.x3 = bf16[2,256,512]{2,1,0:T(8,128)(2,1)S(1)} collective-permute-done((bf16[2,256,512]{2,1,0:T(8,128)(2,1)S(1)}, bf16[2,256,512]{2,1,0:T(8,128)(2,1)S(1)}, u32[]{:S(2)}, u32[]{:S(2)}) %collective-permute-start.4) | collective-permute-done | bytes 524320 | tf_op jit(solution)/shard_map/ppermute | solution.py:400
  135.6 21.3 %collective-permute-done.3.x2 = bf16[2,256,512]{2,1,0:T(8,128)(2,1)S(1)} collective-permute-done((bf16[2,256,512]{2,1,0:T(8,128)(2,1)S(1)}, bf16[2,256,512]{2,1,0:T(8,128)(2,1)S(1)}, u32[]{:S(2)}, u32[]{:S(2)}) %collective-permute-start.3) | collective-permute-done | bytes 524320 | tf_op jit(solution)/shard_map/ppermute | solution.py:400
  156.9 0.8 copy-done.11
  157.7 0.3 collective-permute-start.7
  158.0 2.6 %all-to-all-done.2 = bf16[256,8,512]{2,1,0:T(8,128)(2,1)} async-done(((bf16[256,8,512]{2,1,0:T(8,128)(2,1)}), bf16[256,8,512]{2,1,0:T(8,128)(2,1)}, u32[]{:S(2)}, u32[]{:S(2)}) %all-to-all-start.2) | async-done | bytes 2097184 | tf_op jit(solution)/shard_map/all_to_all | solution.py:420
  160.6 2.5 %collective-permute-done.7.cross_b = bf16[4,640,512]{2,1,0:T(8,128)(2,1)S(1)} collective-permute-done((bf16[4,640,512]{2,1,0:T(8,128)(2,1)}, bf16[4,640,512]{2,1,0:T(8,128)(2,1)S(1)}, u32[]{:S(2)}, u32[]{:S(2)}) %collective-permute-start.7) | collective-permute-done | bytes 2621472 | tf_op jit(solution)/shard_map/ppermute | solution.py:400
  163.2 1.5 copy-done.8
  164.6 21.6 %mlp.1 = bf16[2,256,2048]{2,1,0:T(8,128)(2,1)} custom-call(s32[2]{0:T(128)} %pad_add_fusion.meta, bf16[4,512,512]{2,1,0:T(8,128)(2,1)} %bitcast.5.r_hbm, bf16[2,256,512]{2,1,0:T(8,128)(2,1)} %get-tuple-element.44.x0, bf16[2,256,512]{2,1,0:T(8,128)(2,1)} %collective-permute-done.2.x1, bf16[2,256,512]{2,1,0:T(8,128)(2,1)} %copy-done.11, ...), custom_call_target="tpu_custom_call" | custom-call | flops 11811160064 | bytes 27262976 | tf_op jit(solution)/shard_map/mlp/pallas_call | solution.py:331
  (31 shorter events, 0.2 us)
Async XLA Ops:
  7.1 17.9 %copy-start.6 = (f32[512]{0:T(512)S(1)}, f32[512]{0:T(512)}, u32[]{:S(2)}) copy-start(f32[512]{0:T(512)} %param.13) | copy-start | bytes 6148
  7.1 17.9 %copy-start.7 = (f32[512]{0:T(512)S(1)}, f32[512]{0:T(512)}, u32[]{:S(2)}) copy-start(f32[512]{0:T(512)} %param.12) | copy-start | bytes 6148
  11.4 40.7 %all-to-all-start = ((bf16[64,32,256]{2,1,0:T(8,128)(2,1)}), bf16[64,32,256]{2,1,0:T(8,128)(2,1)S(1)}, u32[]{:S(2)}, u32[]{:S(2)}) async-start(bf16[64,32,256]{2,1,0:T(8,128)(2,1)} %first_mix_0.1), calls=%async_computation | async-start | bytes 2097152 | tf_op jit(solution)/shard_map/all_to_all | solution.py:399
  25.0 73.4 %all-gather.5.cloned.1.call-start = ((), (), s32[]{:S(2)}) async-start(), calls=%async_computation.4 | async-start | bytes 3358720 | tf_op jit(solution)/shard_map/all_gather | solution.py:386
  30.0 29.7 %copy-start.9 = (bf16[640,512]{1,0:T(8,128)(2,1)S(1)}, bf16[640,512]{1,0:T(8,128)(2,1)}, u32[]{:S(2)}) copy-start(bf16[640,512]{1,0:T(8,128)(2,1)} %get-tuple-element.34) | copy-start | bytes 1966084
  30.0 17.1 %collective-permute-start = (bf16[656,512]{1,0:T(8,128)(2,1)}, bf16[656,512]{1,0:T(8,128)(2,1)S(1)}, u32[]{:S(2)}, u32[]{:S(2)}) collective-permute-start(bf16[656,512]{1,0:T(8,128)(2,1)} %get-tuple-element.29), channel_id=1, source_target_pairs={{0,6},{1,7},{2,4},{3,5},{4,2},{5,3},{6,0},{7,1},{8,14},{9,15},{10,... | collective-permute-start | bytes 2015240 | tf_op jit(solution)/shard_map/ppermute | solution.py:400
  47.1 5.0 %copy-start.3 = (bf16[656,512]{1,0:T(8,128)(2,1)}, bf16[656,512]{1,0:T(8,128)(2,1)S(1)}, u32[]{:S(2)}) copy-start(bf16[656,512]{1,0:T(8,128)(2,1)S(1)} %collective-permute-done) | copy-start | bytes 2015236
  52.1 15.2 %copy-start.1 = (bf16[64,32,256]{2,1,0:T(8,128)(2,1)}, bf16[64,32,256]{2,1,0:T(8,128)(2,1)S(1)}, u32[]{:S(2)}) copy-start(bf16[64,32,256]{2,1,0:T(8,128)(2,1)S(1)} %all-to-all-done.r_hbm) | copy-start | bytes 3145732
  52.1 34.3 %all-to-all-start.1 = ((bf16[64,32,256]{2,1,0:T(8,128)(2,1)}), bf16[64,32,256]{2,1,0:T(8,128)(2,1)S(1)}, u32[]{:S(2)}, u32[]{:S(2)}) async-start(bf16[64,32,256]{2,1,0:T(8,128)(2,1)} %first_mix_256.1), calls=%async_computation.1 | async-start | bytes 2097152 | tf_op jit(solution)/shard_map/all_to_all | solution.py:399
  59.6 98.1 %all-gather.3.cloned.1.call-start = ((), (), s32[]{:S(2)}) async-start(), calls=%async_computation.3 | async-start | bytes 3276800 | tf_op jit(solution)/shard_map/all_gather | solution.py:386
  59.6 20.2 %collective-permute-start.1 = (bf16[640,512]{1,0:T(8,128)(2,1)S(1)}, bf16[640,512]{1,0:T(8,128)(2,1)S(1)}, u32[]{:S(2)}, u32[]{:S(2)}) collective-permute-start(bf16[640,512]{1,0:T(8,128)(2,1)S(1)} %copy-done.9), channel_id=1, source_target_pairs={{0,6},{1,7},{2,4},{3,5},{4,2},{5,3},{6,0},{7,1},{8,14},{9,15},{10,... | collective-permute-start | bytes 1966088 | tf_op jit(solution)/shard_map/ppermute | solution.py:400
  79.8 15.8 %copy-start.4 = (bf16[640,512]{1,0:T(8,128)(2,1)}, bf16[640,512]{1,0:T(8,128)(2,1)S(1)}, u32[]{:S(2)}) copy-start(bf16[640,512]{1,0:T(8,128)(2,1)S(1)} %collective-permute-done.1) | copy-start | bytes 1966084
  86.4 1.0 copy-start.2
  92.5 18.0 %copy-start.5 = (s32[2]{0:T(128)S(1)}, s32[2]{0:T(128)}, u32[]{:S(2)}) copy-start(s32[2]{0:T(128)} %pad_add_fusion.meta) | copy-start | bytes 28
  92.5 18.2 %copy-start = (bf16[2,1024,512]{2,1,0:T(8,128)(2,1)S(1)}, bf16[2,1024,512]{2,1,0:T(8,128)(2,1)}, u32[]{:S(2)}) copy-start(bf16[2,1024,512]{2,1,0:T(8,128)(2,1)} %param.9) | copy-start | bytes 6291460
  92.5 65.2 %collective-permute-start.5 = (bf16[4,1296,512]{2,1,0:T(8,128)(2,1)}, bf16[4,1296,512]{2,1,0:T(8,128)(2,1)}, u32[]{:S(2)}, u32[]{:S(2)}) collective-permute-start(bf16[4,1296,512]{2,1,0:T(8,128)(2,1)} %pack.1.own), channel_id=1, source_target_pairs={{0,1},{1,0},{2,3},{3,2},{4,5},{5,4},{6,7},{7,6},{8,9},{9,8},{10,11... | collective-permute-start | bytes 15925256 | tf_op jit(solution)/shard_map/ppermute | solution.py:400
  98.4 59.3 %collective-permute-start.6 = (bf16[4,656,512]{2,1,0:T(8,128)(2,1)}, bf16[4,656,512]{2,1,0:T(8,128)(2,1)}, u32[]{:S(2)}, u32[]{:S(2)}) collective-permute-start(bf16[4,656,512]{2,1,0:T(8,128)(2,1)} %bitcast.29), channel_id=1, source_target_pairs={{0,1},{1,0},{2,3},{3,2},{4,5},{5,4},{6,7},{7,6},{8,9},{9,8},{10,11... | collective-permute-start | bytes 8060936 | tf_op jit(solution)/shard_map/ppermute | solution.py:400
  99.0 61.6 %all-to-all-start.2 = ((bf16[256,8,512]{2,1,0:T(8,128)(2,1)}), bf16[256,8,512]{2,1,0:T(8,128)(2,1)}, u32[]{:S(2)}, u32[]{:S(2)}) async-start(bf16[256,8,512]{2,1,0:T(8,128)(2,1)} %second_mix_256.1), calls=%async_computation.2 | async-start | bytes 4194304 | tf_op jit(solution)/shard_map/all_to_all | solution.py:420
  111.6 24.0 %collective-permute-start.4 = (bf16[2,256,512]{2,1,0:T(8,128)(2,1)S(1)}, bf16[2,256,512]{2,1,0:T(8,128)(2,1)S(1)}, u32[]{:S(2)}, u32[]{:S(2)}) collective-permute-start(bf16[2,256,512]{2,1,0:T(8,128)(2,1)S(1)} %get-tuple-element.51), channel_id=1, source_target_pairs={{0,3},{1,2},{2,1},{3,0},{4,7},{5,6},{6,5},{7,4},{8,11},{9,10},{10,... | collective-permute-start | bytes 1572872 | tf_op jit(solution)/shard_map/ppermute | solution.py:400
  114.7 42.1 %collective-permute-start.3 = (bf16[2,256,512]{2,1,0:T(8,128)(2,1)S(1)}, bf16[2,256,512]{2,1,0:T(8,128)(2,1)S(1)}, u32[]{:S(2)}, u32[]{:S(2)}) collective-permute-start(bf16[2,256,512]{2,1,0:T(8,128)(2,1)S(1)} %get-tuple-element.52), channel_id=1, source_target_pairs={{0,2},{1,3},{2,0},{3,1},{4,6},{5,7},{6,4},{7,5},{8,10},{9,11},{10,... | collective-permute-start | bytes 1572872 | tf_op jit(solution)/shard_map/ppermute | solution.py:400
  116.7 41.1 %collective-permute-start.2 = (bf16[2,256,512]{2,1,0:T(8,128)(2,1)S(1)}, bf16[2,256,512]{2,1,0:T(8,128)(2,1)}, u32[]{:S(2)}, u32[]{:S(2)}) collective-permute-start(bf16[2,256,512]{2,1,0:T(8,128)(2,1)S(1)} %get-tuple-element.53), channel_id=1, source_target_pairs={{0,1},{1,0},{2,3},{3,2},{4,5},{5,4},{6,7},{7,6},{8,9},{9,8},{10,11... | collective-permute-start | bytes 1572872 | tf_op jit(solution)/shard_map/ppermute | solution.py:400
  135.6 27.6 %copy-start.10 = (bf16[2,256,512]{2,1,0:T(8,128)(2,1)}, bf16[2,256,512]{2,1,0:T(8,128)(2,1)S(1)}, u32[]{:S(2)}) copy-start(bf16[2,256,512]{2,1,0:T(8,128)(2,1)S(1)} %collective-permute-done.4.x3) | copy-start | bytes 1572868
  156.9 0.8 copy-start.11
  157.7 5.4 %collective-permute-start.7 = (bf16[4,640,512]{2,1,0:T(8,128)(2,1)}, bf16[4,640,512]{2,1,0:T(8,128)(2,1)S(1)}, u32[]{:S(2)}, u32[]{:S(2)}) collective-permute-start(bf16[4,640,512]{2,1,0:T(8,128)(2,1)} %bitcast.31), channel_id=1, source_target_pairs={{0,1},{1,0},{2,3},{3,2},{4,5},{5,4},{6,7},{7,6},{8,9},{9,8},{10,11... | collective-permute-start | bytes 7864328 | tf_op jit(solution)/shard_map/ppermute | solution.py:400
  163.2 1.5 copy-start.8
Sparse Core Ops, SparseCore 0:
  52.2 46.1 all-gather.4
  100.2 54.5 all-gather.2
